TPU v7x, 256 devices: a whole 4x4x8 slice. The times are simulated.
256 devices in a mesh: seq: 32 (over y, z), head: 8 (over x, core).
Axes of the slice: x: 4, y: 4, z: 8, core: 2. Of those that a mesh axis runs over, the one named last changes fastest.
Arguments:
- queries: bfloat16 [128, 16, 4096], P('seq', None, 'head'), may hold values from -6 to 6
- incoming_key_value: bfloat16 [2, 128, 16, 2048], P(None, 'seq', None, 'head'), may hold values from -6 to 6
- prefix_key_value_pool: bfloat16 [2, 256, 512, 2048], P(None, 'seq', None, 'head'), may hold values from -6 to 6
- response_key_value: bfloat16 [2, 128, 2048, 2048], P(None, 'seq', None, 'head'), may hold values from -6 to 6
- residual: bfloat16 [128, 16, 4608], P('seq', None, 'head')
- lengths: int32 [128], P('seq'), may hold values from 1 to 2048, 131072 in all
- rollout_task_map: int32 [128, 1], replicated, may hold values from 0 to 11; in each aligned block of 128 rows (0 to 127, 128 to 255, ...) at most 22 rows name the same one
- slot_block_table: int32 [256], P('seq'), may hold values from 0 to 255, each once
- output_projection_weight: bfloat16 [4096, 4608], P('head'), may hold values from -0.125 to 0.125
- adapter_down_weight: bfloat16 [4096, 16], P('head'), may hold values from -0.09375 to 0.09375
- adapter_up_weight: bfloat16 [16, 4608], replicated, may hold values from -1.5 to 1.5
- post_norm_gain: float32 [4608], P('head'), may hold values from 0.5 to 1.5
- value_head_weight: float32 [4608], P('head'), may hold values from -0.09375 to 0.09375
Outputs:
- hidden: bfloat16 [128, 16, 4608], P('seq', None, 'head')
- values: float32 [128, 16], P('seq')
Inputs may be any that keep to these rules, and one draw needn't show every extreme that they name: `rollout_task_map`: each task prompt is the prompt of at least one and at most 22 rollouts; some prompt has exactly 22. `lengths`: the largest length is exactly 2048. `slot_block_table`: a permutation; blocks below 64 are the system context, block 64 + p * 16 + j is block j of task prompt p.
All inputs are finite; a program needn't handle non-finite values. No bound on the sum of `lengths` on one device may be relied on, other than what follows from the above.
Results may differ from a plain program's by a relative error of at most 0.0054.
Values may be sent and summed in bfloat16 or wider, within the bound.
A program may use at most 128 MiB of HBM per device.

v0:
```python
import jax
import jax.numpy as jnp
from jax import lax
from jax.sharding import PartitionSpec as P

MODEL_WIDTH = 4608
HEAD_SIZE = 128
PROMPT_BLOCKS = 16


SCALE = 144.0 ** (-0.5)
SOFTCAP = 50.0
EPS = 1e-06


def block_terms(query_rows, block_keys, block_values, visible):
    scores = (
        jnp.einsum("mgqh,kgh->mgqk", query_rows, block_keys, preferred_element_type=jnp.float32)
        * SCALE
    )
    capped = SOFTCAP * jnp.tanh(scores / SOFTCAP)
    weights = jnp.exp(capped)
    if visible is not None:
        weights = jnp.where(visible[:, None, None, :], weights, 0.0)
    weight_sum = jnp.sum(weights, axis=-1)
    weighted = jnp.einsum(
        "mgqk,kgh->mgqh",
        weights.astype(jnp.bfloat16),
        block_values,
        preferred_element_type=jnp.float32,
    )
    return (weighted, weight_sum)


def local(
    queries,
    incoming_key_value,
    prefix_key_value_pool,
    response_key_value,
    residual,
    lengths,
    rollout_task_map,
    slot_block_table,
    output_projection_weight,
    adapter_down_weight,
    adapter_up_weight,
    post_norm_gain,
    value_head_weight,
):
    roll_dev, new_count, query_width = queries.shape
    kv_width = incoming_key_value.shape[-1]
    groups = kv_width // HEAD_SIZE
    per_group = query_width // kv_width
    past_count = response_key_value.shape[2]
    grouped = queries.reshape(roll_dev, new_count, groups, per_group, HEAD_SIZE)
    past_keys = response_key_value[0].reshape(roll_dev, past_count, groups, HEAD_SIZE)
    past_values = response_key_value[1].reshape(roll_dev, past_count, groups, HEAD_SIZE)
    new_keys = incoming_key_value[0].reshape(roll_dev, new_count, groups, HEAD_SIZE)
    new_values = incoming_key_value[1].reshape(roll_dev, new_count, groups, HEAD_SIZE)
    past_positions = jnp.arange(past_count, dtype=jnp.int32)
    new_positions = jnp.arange(new_count, dtype=jnp.int32)
    past_visible = jnp.broadcast_to(
        past_positions[None, None, :] < lengths[:, None, None], (roll_dev, new_count, past_count)
    )
    causal = new_positions[None, :] <= new_positions[:, None]
    past_out, past_sum = jax.vmap(block_terms, in_axes=(0, 0, 0, 0))(
        grouped, past_keys, past_values, past_visible
    )
    own_out, own_sum = jax.vmap(block_terms, in_axes=(0, 0, 0, None))(
        grouped, new_keys, new_values, causal
    )
    gathered = lax.all_gather(queries, "seq", axis=0, tiled=True)
    rollouts = gathered.shape[0]
    seq_size = lax.axis_size("seq")
    sys_blocks = 2 * seq_size
    prompts = 6 * seq_size // PROMPT_BLOCKS
    capacity = 2 * ((rollouts + prompts - 1) // prompts)
    all_queries = gathered.reshape(rollouts, new_count, groups, per_group, HEAD_SIZE)
    flat_queries = all_queries.reshape(rollouts * new_count, groups, per_group, HEAD_SIZE)
    task_ids = rollout_task_map[:, 0]
    rollout_ids = jnp.arange(rollouts, dtype=jnp.int32)
    same_task = task_ids[:, None] == task_ids[None, :]
    task_rank = jnp.sum(
        (same_task & (rollout_ids[None, :] < rollout_ids[:, None])).astype(jnp.int32), axis=1
    )
    placed = (task_ids[None, None, :] == jnp.arange(prompts, dtype=jnp.int32)[:, None, None]) & (
        task_rank[None, None, :] == jnp.arange(capacity, dtype=jnp.int32)[None, :, None]
    )
    placed_count = jnp.sum(placed.astype(jnp.int32), axis=2)
    members = jnp.sum(jnp.where(placed, rollout_ids[None, None, :], 0), axis=2) + rollouts * (
        1 - placed_count
    )
    pool_blocks, block_len = (prefix_key_value_pool.shape[1], prefix_key_value_pool.shape[2])
    pool_keys = prefix_key_value_pool[0].reshape(pool_blocks, block_len, groups, HEAD_SIZE)
    pool_values = prefix_key_value_pool[1].reshape(pool_blocks, block_len, groups, HEAD_SIZE)
    zeros_out = jnp.zeros((rollouts, new_count, groups, per_group, HEAD_SIZE), jnp.float32)
    zeros_sum = jnp.zeros((rollouts, new_count, groups, per_group), jnp.float32)

    def visit(slot_index, totals):
        prefix_out, prefix_sum = totals
        logical = slot_block_table[slot_index]
        block_keys = pool_keys[slot_index]
        block_values = pool_values[slot_index]

        def system_block(running_out, running_sum):
            weighted, weight_sum = block_terms(flat_queries, block_keys, block_values, None)
            return (
                running_out + weighted.reshape(running_out.shape),
                running_sum + weight_sum.reshape(running_sum.shape),
            )

        def prompt_block(running_out, running_sum):
            prompt = jnp.clip((logical - sys_blocks) // PROMPT_BLOCKS, 0, prompts - 1)
            member_rows = members[prompt]
            picked = all_queries[jnp.minimum(member_rows, rollouts - 1)]
            weighted, weight_sum = block_terms(
                picked.reshape(capacity * new_count, groups, per_group, HEAD_SIZE),
                block_keys,
                block_values,
                None,
            )
            running_out = running_out.at[member_rows].add(
                weighted.reshape(capacity, new_count, groups, per_group, HEAD_SIZE), mode="drop"
            )
            running_sum = running_sum.at[member_rows].add(
                weight_sum.reshape(capacity, new_count, groups, per_group), mode="drop"
            )
            return (running_out, running_sum)

        return lax.cond(logical < sys_blocks, system_block, prompt_block, prefix_out, prefix_sum)

    prefix_out, prefix_sum = lax.fori_loop(0, pool_blocks, visit, (zeros_out, zeros_sum))
    summed_out, summed_sum = lax.psum((prefix_out, prefix_sum), "seq")
    start = lax.axis_index("seq") * roll_dev
    mine_out = lax.dynamic_slice_in_dim(summed_out, start, roll_dev, 0)
    mine_sum = lax.dynamic_slice_in_dim(summed_sum, start, roll_dev, 0)
    weighted_all = mine_out + past_out + own_out
    weight_total = mine_sum + past_sum + own_sum
    attention_output = (
        (weighted_all / weight_total[..., None])
        .astype(jnp.bfloat16)
        .reshape(roll_dev * new_count, query_width)
    )
    low_rank_output = jnp.dot(
        attention_output, adapter_down_weight, preferred_element_type=jnp.float32
    )
    partial_out = jnp.dot(
        attention_output, output_projection_weight, preferred_element_type=jnp.float32
    ) + jnp.dot(
        low_rank_output, adapter_up_weight.astype(jnp.float32), precision=lax.Precision.HIGHEST
    )
    projected = lax.psum_scatter(partial_out, "head", scatter_dimension=1, tiled=True)
    squares = lax.psum(jnp.sum(projected * projected, axis=1), "head")
    normed = projected * lax.rsqrt(squares / MODEL_WIDTH + EPS)[:, None] * post_norm_gain
    stream = residual.reshape(roll_dev * new_count, -1).astype(jnp.float32) + normed
    power, along = lax.psum(
        (jnp.sum(stream * stream, axis=1), jnp.sum(stream * value_head_weight, axis=1)), "head"
    )
    value_score = along * lax.rsqrt(power / MODEL_WIDTH + EPS)
    return (
        stream.astype(jnp.bfloat16).reshape(residual.shape),
        value_score.reshape(roll_dev, new_count),
    )


def solution(mesh):
    placed = (
        P("seq", None, "head"),
        P(None, "seq", None, "head"),
        P(None, "seq", None, "head"),
        P(None, "seq", None, "head"),
        P("seq", None, "head"),
        P("seq"),
        P(),
        P("seq"),
        P("head", None),
        P("head", None),
        P(),
        P("head"),
        P("head"),
    )
    return jax.shard_map(
        local,
        mesh=mesh,
        in_specs=placed,
        out_specs=(P("seq", None, "head"), P("seq", None)),
        check_vma=False,
    )
```

profile of v0, /device:TPU:1, one launch (start us, length us, event | category | flops | bytes accessed | tf_op | source)
XLA Modules:
  0.0 535.1 jit_solution(13645803025424036508)
XLA Ops:
  18.8 69.7 %all-gather.2.cloned.1.call-done = bf16[128,16,512]{2,1,0:T(8,128)(2,1)} async-done(((bf16[4,16,512]{2,1,0:T(8,128)(2,1)}), bf16[128,16,512]{2,1,0:T(8,128)(2,1)}) %all-gather.2.cloned.1.call-update) | async-done | bytes 2097168 | tf_op jit(solution)/shard_map/all_gather | solution.py:72
  97.3 140.8 %while.15 = (s32[]{:T(128)}, f32[128,16,2,2,128]{4,1,3,2,0:T(8,128)}, f32[128,16,2,2]{1,3,2,0:T(2,128)S(1)}, s32[8]{0:T(128)S(1)}, bf16[8,512,2,128]{1,3,2,0:T(8...) while((s32[]{:T(128)}, ...), condition=%wide.region_10.11_spmd, body=%wide.region_3.10_spmd.sunk | while | flops 2173698048 | bytes 55312632 | solution.py:132
  100.2 12.8 %conditional.2 = (f32[128,16,2,2,128]{4,1,3,2,0:T(8,128)}, f32[128,16,2,2]{1,3,2,0:T(2,128)S(1)}) conditional(s32[]{:T(128)} %convert_element_type.62, (s32[]{:T(128)}, s32[12,22]{1,0:T(8,128)S(1)}, bf16[128,16,2,2,128]{4,3,2,1,0:T(2,128)(2,1)}, bf16[512,2,128]{2,0,1:T(8,128)(2,1)S(1)}, bf16[512,2,128]{2,0,1:T(8,128)(2,1)S(1)}, ...), branch_computations={%region_4.7_spmd, %region_8.9_spmd} | conditional | flops 2173698048 | bytes 53215248 | solution.py:130
  105.8 5.2 scatter_fusion
  115.6 12.7 %conditional.2 = (f32[128,16,2,2,128]{4,1,3,2,0:T(8,128)}, f32[128,16,2,2]{1,3,2,0:T(2,128)S(1)}) conditional(s32[]{:T(128)} %convert_element_type.62, (s32[]{:T(128)}, s32[12,22]{1,0:T(8,128)S(1)}, bf16[128,16,2,2,128]{4,3,2,1,0:T(2,128)(2,1)}, bf16[512,2,128]{2,0,1:T(8,128)(2,1)S(1)}, bf16[512,2,128]{2,0,1:T(8,128)(2,1)S(1)}, ...), branch_computations={%region_4.7_spmd, %region_8.9_spmd} | conditional | flops 2173698048 | bytes 53215248 | solution.py:130
  131.0 12.7 %conditional.2 = (f32[128,16,2,2,128]{4,1,3,2,0:T(8,128)}, f32[128,16,2,2]{1,3,2,0:T(2,128)S(1)}) conditional(s32[]{:T(128)} %convert_element_type.62, (s32[]{:T(128)}, s32[12,22]{1,0:T(8,128)S(1)}, bf16[128,16,2,2,128]{4,3,2,1,0:T(2,128)(2,1)}, bf16[512,2,128]{2,0,1:T(8,128)(2,1)S(1)}, bf16[512,2,128]{2,0,1:T(8,128)(2,1)S(1)}, ...), branch_computations={%region_4.7_spmd, %region_8.9_spmd} | conditional | flops 2173698048 | bytes 53215248 | solution.py:130
  136.6 5.2 scatter_fusion
  146.4 12.5 %conditional.2 = (f32[128,16,2,2,128]{4,1,3,2,0:T(8,128)}, f32[128,16,2,2]{1,3,2,0:T(2,128)S(1)}) conditional(s32[]{:T(128)} %convert_element_type.62, (s32[]{:T(128)}, s32[12,22]{1,0:T(8,128)S(1)}, bf16[128,16,2,2,128]{4,3,2,1,0:T(2,128)(2,1)}, bf16[512,2,128]{2,0,1:T(8,128)(2,1)S(1)}, bf16[512,2,128]{2,0,1:T(8,128)(2,1)S(1)}, ...), branch_computations={%region_4.7_spmd, %region_8.9_spmd} | conditional | flops 2173698048 | bytes 53215248 | solution.py:130
  161.7 12.4 %conditional.2 = (f32[128,16,2,2,128]{4,1,3,2,0:T(8,128)}, f32[128,16,2,2]{1,3,2,0:T(2,128)S(1)}) conditional(s32[]{:T(128)} %convert_element_type.62, (s32[]{:T(128)}, s32[12,22]{1,0:T(8,128)S(1)}, bf16[128,16,2,2,128]{4,3,2,1,0:T(2,128)(2,1)}, bf16[512,2,128]{2,0,1:T(8,128)(2,1)S(1)}, bf16[512,2,128]{2,0,1:T(8,128)(2,1)S(1)}, ...), branch_computations={%region_4.7_spmd, %region_8.9_spmd} | conditional | flops 2173698048 | bytes 53215248 | solution.py:130
  176.8 30.2 %conditional.2 = (f32[128,16,2,2,128]{4,1,3,2,0:T(8,128)}, f32[128,16,2,2]{1,3,2,0:T(2,128)S(1)}) conditional(s32[]{:T(128)} %convert_element_type.62, (s32[]{:T(128)}, s32[12,22]{1,0:T(8,128)S(1)}, bf16[128,16,2,2,128]{4,3,2,1,0:T(2,128)(2,1)}, bf16[512,2,128]{2,0,1:T(8,128)(2,1)S(1)}, bf16[512,2,128]{2,0,1:T(8,128)(2,1)S(1)}, ...), branch_computations={%region_4.7_spmd, %region_8.9_spmd} | conditional | flops 2173698048 | bytes 53215248 | solution.py:130
  176.8 10.2 %bitcast_reduce_fusion = (f32[2048,2,2]{0,2,1:T(2,128)S(1)}, f32[2,512,2048,2]{2,1,3,0:T(8,128)}) fusion(bf16[2048,2,2,128]{3,2,1,0:T(2,128)(2,1)} %get-tuple-element.241, bf16[512,2,128]{2,0,1:T(8,128)(2,1)S(1)} %get-tuple-element.179), kind=kOutput, calls=%fused_computation.3 | convolution fusion | flops 1086316544 | bytes 19169280 | tf_op jit(solution)/shard_map/while/body/eval_jaxpr/cond/branch_1_fun/mgqh,kgh->mgqk/dot_general | solution.py:18
  187.0 13.0 %fusion = f32[2,2048,2,128]{3,1,2,0:T(8,128)} fusion(f32[2,512,2048,2]{2,1,3,0:T(8,128)} %get-tuple-element.279, bf16[512,2,128]{2,0,1:T(8,128)(2,1)S(1)} %get-tuple-element.181), kind=kOutput, calls=%fused_computation.6 | convolution fusion | flops 1086324736 | bytes 21233664 | tf_op jit(solution)/shard_map/while/body/eval_jaxpr/cond/branch_1_fun/mgqk,kgh->mgqh/dot_general | solution.py:26
  200.0 6.6 %copy_add_fusion = f32[128,16,2,2,128]{4,1,3,2,0:T(8,128)} fusion(f32[128,16,2,2,128]{4,1,3,2,0:T(8,128)} %get-tuple-element.178, f32[128,16,2,2,128]{4,1,0,3,2:T(8,128)} %bitcast.120), kind=kLoop, calls=%fused_computation.7 | loop fusion | flops 1048576 | bytes 12582912 | tf_op jit(solution)/shard_map/while/body/eval_jaxpr/cond/branch_1_fun/add | solution.py:108
  209.6 12.8 %conditional.2 = (f32[128,16,2,2,128]{4,1,3,2,0:T(8,128)}, f32[128,16,2,2]{1,3,2,0:T(2,128)S(1)}) conditional(s32[]{:T(128)} %convert_element_type.62, (s32[]{:T(128)}, s32[12,22]{1,0:T(8,128)S(1)}, bf16[128,16,2,2,128]{4,3,2,1,0:T(2,128)(2,1)}, bf16[512,2,128]{2,0,1:T(8,128)(2,1)S(1)}, bf16[512,2,128]{2,0,1:T(8,128)(2,1)S(1)}, ...), branch_computations={%region_4.7_spmd, %region_8.9_spmd} | conditional | flops 2173698048 | bytes 53215248 | solution.py:130
  215.2 5.2 scatter_fusion
  225.1 12.7 %conditional.2 = (f32[128,16,2,2,128]{4,1,3,2,0:T(8,128)}, f32[128,16,2,2]{1,3,2,0:T(2,128)S(1)}) conditional(s32[]{:T(128)} %convert_element_type.62, (s32[]{:T(128)}, s32[12,22]{1,0:T(8,128)S(1)}, bf16[128,16,2,2,128]{4,3,2,1,0:T(2,128)(2,1)}, bf16[512,2,128]{2,0,1:T(8,128)(2,1)S(1)}, bf16[512,2,128]{2,0,1:T(8,128)(2,1)S(1)}, ...), branch_computations={%region_4.7_spmd, %region_8.9_spmd} | conditional | flops 2173698048 | bytes 53215248 | solution.py:130
  238.9 5.8 %fusion.42 = (bf16[1,4,2048,256]{3,2,1,0:T(8,128)(2,1)}, bf16[1,4,2048,256]{3,2,1,0:T(8,128)(2,1)}) fusion(bf16[2,4,2048,256]{3,2,1,0:T(8,128)(2,1)} %param.20), kind=kLoop, calls=%fused_computation.81 | loop fusion | bytes 16777216 | tf_op jit(solution)/shard_map/slice | solution.py:56
  244.7 6.3 %copy.113 = bf16[1,4,2048,256]{2,3,1,0:T(8,128)(2,1)} copy(bf16[1,4,2048,256]{3,2,1,0:T(8,128)(2,1)} %get-tuple-element.286) | data formatting | bytes 8388608
  251.1 6.4 %copy.114 = bf16[1,4,2048,256]{2,3,1,0:T(8,128)(2,1)} copy(bf16[1,4,2048,256]{3,2,1,0:T(8,128)(2,1)} %get-tuple-element.287) | data formatting | bytes 8388608
  261.4 165.3 %psum.36 = f32[128,16,2,2]{1,3,2,0:T(2,128)S(1)} all-reduce(f32[128,16,2,2]{1,3,2,0:T(2,128)S(1)} %get-tuple-element.200), channel_id=1, replica_groups=mesh['seq'=32,'head'=8] {'seq'}, use_global_device_ids=true, to_apply=%region_12.13 | all-reduce | flops 8192 | bytes 65536 | tf_op jit(solution)/shard_map/psum | solution.py:133
  426.6 27.2 %all-reduce.3.cloned.1.call-done = f32[128,16,2,2,128]{4,1,3,2,0:T(8,128)} async-done(((f32[128,16,2,2,128]{4,1,3,2,0:T(8,128)}), f32[128,16,2,2,128]{4,1,3,2,0:T(8,128)}) %all-reduce.3.cloned.1.call-update) | async-done | bytes 4194320 | tf_op jit(solution)/shard_map/psum | solution.py:133
  463.8 33.9 %reduce-scatter.4.cloned.1.call-done = f32[576,64]{1,0:T(8,128)} async-done(((f32[4608,64]{1,0:T(8,128)}), f32[576,64]{1,0:T(8,128)}) %reduce-scatter.4.cloned.1.call-update) | async-done | bytes 147472
  498.9 15.1 %psum.37 = f32[64]{0:T(128)S(1)} all-reduce(f32[64]{0:T(128)S(1)} %multiply_reduce_fusion.2), channel_id=1, replica_groups=mesh['seq'=32,'head'=8] {'head'}, use_global_device_ids=true, to_apply=%region_17.18 | all-reduce | flops 64 | bytes 512 | tf_op jit(solution)/shard_map/psum | solution.py:153
  514.8 13.1 %all-reduce = (f32[64]{0:T(128)S(1)}, f32[64]{0:T(128)S(1)}) all-reduce(f32[64]{0:T(128)S(1)} %get-tuple-element.255, f32[64]{0:T(128)S(1)} %get-tuple-element.254), channel_id=1, replica_groups=mesh['seq'=32,'head'=8] {'head'}, use_global_device_ids=true, to_apply=%region_19.20 | all-reduce | flops 128 | bytes 1024 | tf_op jit(solution)/shard_map/psum | solution.py:156
  (165 shorter events, 121.8 us)
Async XLA Ops:
  7.2 454.0 %copy-start = (bf16[16,4608]{1,0:T(8,128)(2,1)S(1)}, bf16[16,4608]{1,0:T(8,128)(2,1)}, u32[]{:S(2)}) copy-start(bf16[16,4608]{1,0:T(8,128)(2,1)} %param.27) | copy-start | bytes 442372
  7.2 81.3 %all-gather.2.cloned.1.call-start = ((), (), s32[]{:S(2)}) async-start(), calls=%async_computation.1 | async-start | bytes 2162688 | tf_op jit(solution)/shard_map/all_gather | solution.py:72
  7.9 446.0 %all-reduce.3.cloned.1.call-start = ((), (), s32[]{:S(2)}) async-start(), calls=%async_computation.2 | async-start | bytes 8388608 | tf_op jit(solution)/shard_map/psum | solution.py:133
  11.8 6.3 %copy-start.8 = (s32[128,1]{0,1:T(1,128)S(1)}, s32[128,1]{0,1:T(1,128)}, u32[]{:S(2)}) copy-start(s32[128,1]{0,1:T(1,128)} %param.23) | copy-start | bytes 1540
  88.5 4.1 copy-start.1
  92.6 4.6 copy-start.10
  238.1 0.8 copy-start.2
  238.1 259.5 %reduce-scatter.4.cloned.1.call-start = ((), (), s32[]{:S(2)}) async-start(), calls=%async_computation.3 | async-start | bytes 2654208
  244.7 6.3 %copy-start.4 = (bf16[2,4,16,256]{3,2,1,0:T(8,128)(2,1)S(1)}, bf16[2,4,16,256]{3,2,1,0:T(8,128)(2,1)}, u32[]{:S(2)}) copy-start(bf16[2,4,16,256]{3,2,1,0:T(8,128)(2,1)} %param.18) | copy-start | bytes 196612
  251.1 6.9 %copy-start.9 = (s32[4]{0:T(128)S(1)}, s32[4]{0:T(128)}, u32[]{:S(2)}) copy-start(s32[4]{0:T(128)} %param.22) | copy-start | bytes 52
  457.6 3.4 copy-start.5
  461.1 52.8 %copy-start.3 = (bf16[4,16,576]{2,1,0:T(8,128)(2,1)S(1)}, bf16[4,16,576]{2,1,0:T(8,128)(2,1)}, u32[]{:S(2)}) copy-start(bf16[4,16,576]{2,1,0:T(8,128)(2,1)} %param.21) | copy-start | bytes 221188
  461.1 52.8 %copy-start.6 = (f32[576]{0:T(1024)S(1)}, f32[576]{0:T(1024)}, u32[]{:S(2)}) copy-start(f32[576]{0:T(1024)} %param.28) | copy-start | bytes 6916
  461.1 52.8 %copy-start.7 = (f32[576]{0:T(1024)S(1)}, f32[576]{0:T(1024)}, u32[]{:S(2)}) copy-start(f32[576]{0:T(1024)} %param.29) | copy-start | bytes 6916
Sparse Core Ops, SparseCore 0:
  10.6 77.8 all-gather.1
  238.2 215.5 all-reduce.2
  463.9 33.6 reduce-scatter.3
where the time goes:
time: 538 us; the launch traced here: 535 us
  blocking collectives  193 us (36%)
  waiting for transfers between devices  131 us (24%)
  local copies, waits for them, and re-layouts  79.7 us (15%)
  other arithmetic  56.9 us (11%)
  matrix products  48.2 us (9%)
  between operations  14 us (3%)
  loops' own time  11.3 us (2%)
    psum x1, blocking collectives, local(): summed_out, summed_sum = lax.psum((prefix_out, prefix_sum), 'seq')  165 us
    all_gather x1, waiting for transfers between devices, local(): gathered = lax.all_gather(queries, 'seq', axis=0, tiled=True)  69.7 us
    scatter-add x7, other arithmetic, prompt_block(): running_out.at[member_rows]  35.6 us
    unnamed x4, waiting for transfers between devices  34.6 us
    psum x1, waiting for transfers between devices, local(): summed_out, summed_sum = lax.psum((prefix_out, prefix_sum), 'seq')  27.2 us
    dot_general x10, matrix products, block_terms(): jnp.einsum('mgqk,kgh->mgqh', weights.astype(jnp.bfloat16), block_values,...  23.1 us
    unnamed x28, local copies, waits for them, and re-layouts  22.8 us
    dot_general x10, matrix products, block_terms(): jnp.einsum('mgqh,kgh->mgqk', query_rows, block_keys, preferred_element_ty...  21 us
  transfers between devices with their start and end apart: 3, of which 3 were waited for; matrix products, arithmetic and copies ran while one was open for 6% of the time, Pallas kernels for 0%

commit v1 on v0

v1 whole, which is shorter than its diff:
```python
import functools

import jax
import jax.numpy as jnp
from jax import lax
from jax.experimental import pallas as pl
from jax.experimental.pallas import tpu as pltpu
from jax.sharding import PartitionSpec as P

MODEL_WIDTH = 4608
HEAD = 128
PROMPT_BLOCKS = 16
EPS = 1e-06
C1 = 144.0 ** (-0.5) / 50.0
C2 = 50.0 * 1.4426950408889634

NY, NZ, NH = 4, 8, 8
ROWS = 64
WIDTH = 512
HEADS = 4
CHUNK = 576
PADDED = 640
MIB = 1 << 20
MESH = pl.DeviceIdType.MESH
F32 = jnp.float32
BF16 = jnp.bfloat16


def weight_of(scores):
    return jnp.exp2(jnp.tanh(scores * C1) * C2)


def dot_t(a, b):
    return lax.dot_general(a, b, (((1,), (1,)), ((), ())), preferred_element_type=F32)


def dot(a, b):
    return jnp.dot(a, b, preferred_element_type=F32)


def lane_sum(p):
    total = p[:, :HEAD]
    for i in range(1, p.shape[1] // HEAD):
        total = total + p[:, i * HEAD : (i + 1) * HEAD]
    return total


def position():
    seq = lax.axis_index("seq")
    head = lax.axis_index("head")
    return lax.div(seq, NZ), lax.rem(seq, NZ), head


def wrap(v, n):
    return lax.rem(v + 2 * n, n)


def shifted(y, z, head, axis, step):
    if axis == 0:
        return (wrap(y + step, NY) * NZ + z, head)
    return (y * NZ + wrap(z + step, NZ), head)


def cols(h):
    return slice(h * HEAD, (h + 1) * HEAD)


def gather_kernel(
    len_ref, q_ref, inc_ref, resp_ref, qall, oloc, lloc, cache, load_sem, s1, r1, s2, r2
):
    y, z, head = position()
    loads = []
    for i in range(4):
        c = pltpu.make_async_copy(resp_ref.at[:, i], cache.at[i], load_sem.at[i])
        c.start()
        loads.append(c)

    barrier = pltpu.get_barrier_semaphore()
    for axis in (0, 1):
        for step in (1, -1):
            pl.semaphore_signal(
                barrier, inc=1, device_id=shifted(y, z, head, axis, step), device_id_type=MESH
            )
    qall[y, z] = q_ref[...]
    pl.semaphore_wait(barrier, 4)

    def attend(i):
        loads[i].wait()
        length = len_ref[i]
        rows = slice(i * 16, (i + 1) * 16)
        for g in range(2):
            lhs = jnp.concatenate([q_ref[rows, cols(2 * g)], q_ref[rows, cols(2 * g + 1)]], axis=0)
            out = jnp.zeros((32, HEAD), F32)
            total = jnp.zeros((32, HEAD), F32)
            for part in range(4):
                at = slice(part * 512, (part + 1) * 512)
                p = weight_of(dot_t(lhs, cache[i, 0, at, cols(g)]))
                where = lax.broadcasted_iota(jnp.int32, p.shape, 1) + part * 512
                p = jnp.where(where < length, p, 0.0)
                total = total + lane_sum(p)
                out = out + dot(p.astype(BF16), cache[i, 1, at, cols(g)])
            p = weight_of(dot_t(lhs, inc_ref[0, i, :, cols(g)]))
            n = lax.rem(lax.broadcasted_iota(jnp.int32, p.shape, 0), 16)
            m = lax.broadcasted_iota(jnp.int32, p.shape, 1)
            p = jnp.where(m <= n, p, 0.0)
            out = out + dot(p.astype(BF16), inc_ref[1, i, :, cols(g)])
            sums = jnp.sum(total, axis=1, keepdims=True) + jnp.sum(p, axis=1, keepdims=True)
            wide = jnp.broadcast_to(sums, (32, HEAD))
            for j in range(2):
                oloc[rows, cols(2 * g + j)] = out[j * 16 : (j + 1) * 16]
                lloc[rows, cols(2 * g + j)] = wide[j * 16 : (j + 1) * 16]

    def run(axis1):
        axis2 = 1 - axis1
        n1, n2 = (NY, NZ) if axis1 == 0 else (NZ, NY)
        c1, c2 = (y, z) if axis1 == 0 else (z, y)
        h1, h2 = n1 // 2, n2 // 2

        def piece(i1, i2, part):
            a, b = (i1, i2) if axis1 == 0 else (i2, i1)
            view = qall.at[a, b]
            if part is None:
                return view
            return view.at[pl.ds(part * (ROWS // 2), ROWS // 2)]

        def first(d, k):
            s = 1 - 2 * d
            view = piece(wrap(c1 - s * k, n1), c2, d if k == h1 - 1 else None)
            return pltpu.make_async_remote_copy(
                src_ref=view,
                dst_ref=view,
                send_sem=s1.at[d, k],
                recv_sem=r1.at[d, k],
                device_id=shifted(y, z, head, axis1, s),
                device_id_type=MESH,
            )

        offsets = [0]
        for k in range(1, h1):
            offsets += [-k, k]
        offsets.append(h1)

        def second(j, d, k):
            s = 1 - 2 * d
            view = piece(wrap(c1 + offsets[j], n1), wrap(c2 - s * k, n2), d if k == h2 - 1 else None)
            return pltpu.make_async_remote_copy(
                src_ref=view,
                dst_ref=view,
                send_sem=s2.at[d, j, k],
                recv_sem=r2.at[d, j, k],
                device_id=shifted(y, z, head, axis2, s),
                device_id_type=MESH,
            )

        pending = list(range(4))
        sent = []

        def go(copy):
            copy.start()
            sent.append(copy)

        for d in (0, 1):
            go(first(d, 0))
        for d in (0, 1):
            go(second(0, d, 0))
        for k in range(h1):
            if pending and k < 1:
                attend(pending.pop(0))
            for d in (0, 1):
                first(d, k).wait_recv()
                if k < h1 - 1:
                    go(first(d, k + 1))
            if k < h1 - 1:
                for d in (0, 1):
                    j = 1 + 2 * k + d
                    for e in (0, 1):
                        go(second(j, e, 0))
            else:
                for e in (0, 1):
                    go(second(n1 - 1, e, 0))
        for k in range(h2):
            for j in range(n1):
                if pending and j % 2 == 1:
                    attend(pending.pop(0))
                for d in (0, 1):
                    second(j, d, k).wait_recv()
                    if k < h2 - 1:
                        go(second(j, d, k + 1))
        for i in pending:
            attend(i)
        for copy in sent:
            copy.wait_send()

    core = lax.rem(head, 2)

    @pl.when(core == 0)
    def _():
        run(0)

    @pl.when(core == 1)
    def _():
        run(1)


def prefix_kernel(rc, map_ref, slot_ref, q_ref, pool_ref, o_ref, l_ref, acc, lanes, sbuf, qbuf, obuf, lbuf, lists, counts, system, meta):
    prompts = counts.shape[0]
    capacity = lists.shape[1]
    rollouts = map_ref.shape[0]
    slots = slot_ref.shape[0]
    sys_blocks = meta
    total_rows = q_ref.shape[0]
    chunks = total_rows // rc

    def note(i, n):
        is_sys = slot_ref[i] < sys_blocks

        @pl.when(is_sys)
        def _():
            system[n] = i

        return n + is_sys.astype(jnp.int32)

    count = lax.fori_loop(0, slots, note, 0)

    def clear(i, _):
        counts[i] = 0
        return 0

    lax.fori_loop(0, prompts, clear, 0)

    def member(r, _):
        p = map_ref[r]
        n = counts[p]
        lists[p, n] = r
        counts[p] = n + 1
        return 0

    lax.fori_loop(0, rollouts, member, 0)

    def rows_of(c):
        return pl.ds(pl.multiple_of(c * rc, rc), rc)

    def score(item, h):
        c = lax.div(item, count)
        b = system[lax.rem(item, count)]
        return dot_t(q_ref[rows_of(c), cols(h)], pool_ref[0, b, :, cols(h // 2)])

    @pl.when(count == 0)
    def _():
        acc[...] = jnp.zeros_like(acc)
        lanes[...] = jnp.zeros_like(lanes)

    @pl.when(count > 0)
    def _():
        items = count * chunks
        sbuf[0] = score(0, 0)

        def step(item, _):
            rows = rows_of(lax.div(item, count))
            turn = lax.rem(item, count)
            b = system[turn]
            first = turn == 0
            following = jnp.minimum(item + 1, items - 1)
            for h in range(HEADS):
                if h < HEADS - 1:
                    sbuf[(h + 1) % 2] = score(item, h + 1)
                else:
                    sbuf[0] = score(following, 0)
                p = weight_of(sbuf[h % 2])
                part = lane_sum(p)
                out = dot(p.astype(BF16), pool_ref[1, b, :, cols(h // 2)])
                lanes[rows, cols(h)] = jnp.where(first, 0.0, lanes[rows, cols(h)]) + part
                acc[rows, cols(h)] = jnp.where(first, 0.0, acc[rows, cols(h)]) + out
            return 0

        lax.fori_loop(0, items, step, 0)

    def prompt_slot(i, _):
        logical = slot_ref[i]

        @pl.when(logical >= sys_blocks)
        def _():
            p = lax.div(logical - sys_blocks, PROMPT_BLOCKS)
            n = counts[p]

            def pick(m, _):
                r = lists[p, m]
                qbuf[pl.ds(pl.multiple_of(m * 16, 16), 16), :] = q_ref[
                    pl.ds(pl.multiple_of(r * 16, 16), 16), :
                ]
                return 0

            lax.fori_loop(0, n, pick, 0)

            def part(c, _):
                rows = pl.ds(pl.multiple_of(c * 128, 128), 128)
                for h in range(HEADS):
                    w = weight_of(dot_t(qbuf[rows, cols(h)], pool_ref[0, i, :, cols(h // 2)]))
                    lbuf[rows, cols(h)] = lane_sum(w)
                    obuf[rows, cols(h)] = dot(w.astype(BF16), pool_ref[1, i, :, cols(h // 2)])
                return 0

            lax.fori_loop(0, lax.div(n + 7, 8), part, 0)

            def put(m, _):
                r = lists[p, m]
                at = pl.ds(pl.multiple_of(r * 16, 16), 16)
                src = pl.ds(pl.multiple_of(m * 16, 16), 16)
                acc[at, :] += obuf[src, :]
                lanes[at, :] += lbuf[src, :]
                return 0

            lax.fori_loop(0, n, put, 0)

        return 0

    lax.fori_loop(0, slots, prompt_slot, 0)

    lane = lax.broadcasted_iota(jnp.int32, (8, WIDTH), 1)
    row = lax.broadcasted_iota(jnp.int32, (8, WIDTH), 0)
    pick_head = jnp.where(lax.div(lane, HEAD) == row, 1.0, 0.0).astype(BF16)

    def finish(d, _):
        at = pl.ds(pl.multiple_of(d * ROWS, ROWS), ROWS)
        o_ref[at, :] = acc[at, :].astype(BF16)
        v = lanes[at, :]
        hi = v.astype(BF16)
        lo = (v - hi.astype(F32)).astype(BF16)
        l_ref[d] = jnp.zeros((8, HEAD), F32)
        l_ref[d, :, :ROWS] = dot_t(pick_head, hi) + dot_t(pick_head, lo)
        return 0

    lax.fori_loop(0, total_rows // ROWS, finish, 0)


def finish_kernel(
    o_ref, l_ref, oloc, lloc, res_ref, w_ref, down_ref, up_ref, gain_ref, vhw_ref,
    hid_ref, val_ref,
    wbuf, part1, lpart1, mine, pmine, rbuf, rlbuf, rbuf2, rlbuf2, chunk, rchunk, small, rsmall,
    w_sem, s1, r1, t1, u1, s2, r2, t2, u2, hs, hr, ss, sr,
):
    y, z, head = position()
    wcopy = pltpu.make_async_copy(w_ref, wbuf, w_sem)
    wcopy.start()

    barrier = pltpu.get_barrier_semaphore()
    for axis in (0, 1):
        for step in (1, -1):
            pl.semaphore_signal(
                barrier, inc=1, device_id=shifted(y, z, head, axis, step), device_id_type=MESH
            )
    seq = y * NZ + z
    for t in range(1, NH):
        pl.semaphore_signal(
            barrier, inc=1, device_id=(seq, wrap(head + t, NH)), device_id_type=MESH
        )
    pl.semaphore_wait(barrier, 4 + NH - 1)

    half = ROWS // 2

    def reduce(axis, n, c, pieces, own, own_l, rb, rl, ss_, rs_, ts_, us_, final, final_l):
        h = n // 2
        sent = []

        def side(view, d):
            return view.at[pl.ds(d * half, half)]

        def copy(d, k, j):
            s = 1 - 2 * d
            if k == 0:
                src = side(own(wrap(c + s * h, n), j), d)
                dst = side(rb.at[d, 0, j], d)
            else:
                src = rb.at[d, k - 1, j]
                dst = rb.at[d, k, j]
            return pltpu.make_async_remote_copy(
                src_ref=src, dst_ref=dst, send_sem=ss_.at[d, k, j], recv_sem=rs_.at[d, k, j],
                device_id=shifted(y, z, head, axis, s), device_id_type=MESH,
            )

        def copy_l(d, k):
            s = 1 - 2 * d
            src = own_l(wrap(c + s * (h if d == 0 else h - 1), n)) if k == 0 else rl.at[d, k - 1]
            return pltpu.make_async_remote_copy(
                src_ref=src, dst_ref=rl.at[d, k], send_sem=ts_.at[d, k], recv_sem=us_.at[d, k],
                device_id=shifted(y, z, head, axis, s), device_id_type=MESH,
            )

        def go(x):
            x.start()
            sent.append(x)

        steps_l = (h, h - 1)
        for j in range(pieces):
            for d in (0, 1):
                go(copy(d, 0, j))
            if j == 0:
                for d in (0, 1):
                    go(copy_l(d, 0))
        for k in range(1, h):
            for j in range(pieces):
                for d in (0, 1):
                    s = 1 - 2 * d
                    copy(d, k - 1, j).wait_recv()
                    mine_here = own(wrap(c + s * (h - k), n), j)
                    if k == 1:
                        a = pl.ds(d * half, half)
                        b = pl.ds((1 - d) * half, half)
                        rb[d, 0, j, a] = (rb[d, 0, j, a].astype(F32) + mine_here[a].astype(F32)).astype(BF16)
                        rb[d, 0, j, b] = mine_here[b]
                    else:
                        rb[d, k - 1, j] = (rb[d, k - 1, j].astype(F32) + mine_here[...].astype(F32)).astype(BF16)
                    go(copy(d, k, j))
                if j == 0:
                    for d in (0, 1):
                        if k < steps_l[d]:
                            s = 1 - 2 * d
                            copy_l(d, k - 1).wait_recv()
                            rl[d, k - 1] = rl[d, k - 1] + own_l(wrap(c + s * (steps_l[d] - k), n))[...]
                            go(copy_l(d, k))
        for j in range(pieces):
            for d in (0, 1):
                copy(d, h - 1, j).wait_recv()
            final(j, own(c, j)[...].astype(F32) + rb[0, h - 1, j].astype(F32) + rb[1, h - 1, j].astype(F32))
            if j == 0:
                for d in (0, 1):
                    copy_l(d, steps_l[d] - 1).wait_recv()
                final_l(own_l(c)[...] + rl[0, steps_l[0] - 1] + rl[1, steps_l[1] - 1])
        for x in sent:
            x.wait_send()

    def run(axis1):
        axis2 = 1 - axis1
        n1, n2 = (NY, NZ) if axis1 == 0 else (NZ, NY)
        c1, c2 = (y, z) if axis1 == 0 else (z, y)

        def own(i, j):
            return o_ref.at[i, j] if axis1 == 0 else o_ref.at[j, i]

        def own_l(i):
            return l_ref.at[i] if axis1 == 0 else l_ref.at[:, i]

        def keep(j, v):
            part1[j] = v.astype(BF16)

            @pl.when(c2 == j)
            def _():
                mine[...] = v

        def keep_l(v):
            lpart1[pl.ds(0, n2)] = v

        reduce(
            axis1, n1, c1, n2, own, own_l,
            rbuf_view(n1, n2),
            rlbuf_view(n1, n2), s1, r1, t1, u1, keep, keep_l,
        )

        def own2(i, j):
            return part1.at[i]

        def own2_l(i):
            return lpart1.at[i]

        def keep2(j, v):
            mine[...] = v - part1[c2].astype(F32) + mine[...]

        def keep2_l(v):
            small[...] = v

        reduce(axis2, n2, c2, 1, own2, own2_l, rbuf2, rlbuf2, s2, r2, t2, u2, keep2, keep2_l)

    def rbuf_view(n1, n2):
        return rbuf[0] if n1 == NY else rbuf[1]

    def rlbuf_view(n1, n2):
        return rlbuf[0] if n1 == NY else rlbuf[1]

    core = lax.rem(head, 2)

    @pl.when(core == 0)
    def _():
        run(1)

    @pl.when(core == 1)
    def _():
        run(0)

    sums = jnp.transpose(jnp.concatenate([small[...], jnp.zeros((HEAD - 8, HEAD), F32)], axis=0))
    att = []
    for h in range(HEADS):
        den = sums[:ROWS, h : h + 1] + lloc[:, cols(h)]
        att.append(((mine[:, cols(h)] + oloc[:, cols(h)]) / den).astype(BF16))
    att = jnp.concatenate(att, axis=1)
    low = dot(att, down_ref[...])
    low_hi = low.astype(BF16)
    low_lo = (low - low_hi.astype(F32)).astype(BF16)
    low_lo2 = (low - low_hi.astype(F32) - low_lo.astype(F32)).astype(BF16)
    wcopy.wait()
    for j in range(NH):
        a = (j * CHUNK) // HEAD * HEAD
        b = a + PADDED
        v = dot(att, wbuf[:, a:b])
        u = up_ref[:, a:b]
        v = v + (dot(low_hi, u) + dot(low_lo, u) + dot(low_lo2, u))
        chunk[j] = v[:, j * CHUNK - a : j * CHUNK - a + CHUNK].astype(BF16)

        @pl.when(head == j)
        def _():
            pmine[...] = v[:, j * CHUNK - a : j * CHUNK - a + CHUNK]

    sends = []
    for t in range(1, NH):
        to = wrap(head + t, NH)
        x = pltpu.make_async_remote_copy(
            src_ref=chunk.at[to], dst_ref=rchunk.at[t - 1], send_sem=hs.at[t - 1], recv_sem=hr.at[t - 1],
            device_id=(seq, to), device_id_type=MESH,
        )
        x.start()
        sends.append(x)
    p = pmine[...]
    for t in range(1, NH):
        sends[t - 1].wait_recv()
        p = p + rchunk[t - 1].astype(F32)

    res = res_ref[...].astype(F32)
    gain = gain_ref[...]
    vhw = vhw_ref[...]
    pg = p * gain
    parts = [p * p, res * res, res * pg, pg * pg, res * vhw, pg * vhw]
    lane = lax.broadcasted_iota(jnp.int32, (ROWS, HEAD), 1)
    packed = jnp.zeros((ROWS, HEAD), F32)
    for i, v in enumerate(parts):
        packed = jnp.where(lane == i, jnp.sum(v, axis=1, keepdims=True), packed)
    packed = jnp.concatenate([packed, jnp.zeros((HEAD - ROWS, HEAD), F32)], axis=0)
    small[...] = jnp.transpose(packed)[:8]
    sends2 = []
    for t in range(1, NH):
        x = pltpu.make_async_remote_copy(
            src_ref=small, dst_ref=rsmall.at[t - 1], send_sem=ss.at[t - 1], recv_sem=sr.at[t - 1],
            device_id=(seq, wrap(head + t, NH)), device_id_type=MESH,
        )
        x.start()
        sends2.append(x)
    total = small[...]
    for t in range(1, NH):
        sends2[t - 1].wait_recv()
        total = total + rsmall[t - 1]
    sq, res2, rpg, pg2, rw, pgw = [total[i : i + 1] for i in range(6)]
    r = lax.rsqrt(sq / MODEL_WIDTH + EPS)
    power = res2 + 2.0 * r * rpg + r * r * pg2
    value = (rw + r * pgw) * lax.rsqrt(power / MODEL_WIDTH + EPS)
    for i in range(4):
        val_ref[i : i + 1, :] = value[:, i * 16 : (i + 1) * 16]
    rcol = jnp.transpose(jnp.broadcast_to(r, (HEAD, HEAD)))[:ROWS, :1]
    hid_ref[...] = (res + pg * rcol).astype(BF16)
    for x in sends + sends2:
        x.wait_send()


def finish_entry(*refs):
    refs = list(refs)
    ins, outs = refs[:10], refs[10:12]
    s = refs[12:]
    wbuf, part1, lpart1, mine, pmine, rb_y, rb_z, rl_y, rl_z = s[:9]
    finish_kernel(
        *ins, *outs, wbuf, part1, lpart1, mine, pmine, (rb_y, rb_z), (rl_y, rl_z), *s[9:]
    )


def local(
    queries, incoming_key_value, prefix_key_value_pool, response_key_value, residual, lengths,
    rollout_task_map, slot_block_table, output_projection_weight, adapter_down_weight,
    adapter_up_weight, post_norm_gain, value_head_weight,
):
    vmem = pl.BlockSpec(memory_space=pltpu.VMEM)
    smem = pl.BlockSpec(memory_space=pltpu.SMEM)
    anyw = pl.BlockSpec(memory_space=pl.ANY)
    dma = pltpu.SemaphoreType.DMA
    sds = jax.ShapeDtypeStruct
    devices = NY * NZ
    rows_all = devices * ROWS

    qall, oloc, lloc = pl.pallas_call(
        gather_kernel,
        out_shape=(
            sds((NY, NZ, ROWS, WIDTH), BF16),
            sds((ROWS, WIDTH), F32),
            sds((ROWS, WIDTH), F32),
        ),
        in_specs=[smem, vmem, vmem, anyw],
        out_specs=(vmem, vmem, vmem),
        scratch_shapes=[
            pltpu.VMEM((4, 2, 2048, 256), BF16),
            dma((4,)),
            dma((2, NZ // 2)),
            dma((2, NZ // 2)),
            dma((2, NZ, NZ // 2)),
            dma((2, NZ, NZ // 2)),
        ],
        compiler_params=pltpu.CompilerParams(
            collective_id=0, has_side_effects=True, vmem_limit_bytes=40 * MIB
        ),
        name="gather_queries",
    )(lengths, queries.reshape(ROWS, WIDTH), incoming_key_value, response_key_value)

    rc = 1024
    prompts = 12
    o, l = pl.pallas_call(
        functools.partial(prefix_kernel_entry, rc),
        out_shape=(sds((rows_all, WIDTH), BF16), sds((devices, 8, HEAD), F32)),
        in_specs=[smem, smem, vmem, vmem],
        out_specs=(vmem, vmem),
        scratch_shapes=[
            pltpu.VMEM((rows_all, WIDTH), F32),
            pltpu.VMEM((rows_all, WIDTH), F32),
            pltpu.VMEM((2, rc, 512), F32),
            pltpu.VMEM((384, WIDTH), BF16),
            pltpu.VMEM((384, WIDTH), F32),
            pltpu.VMEM((384, WIDTH), F32),
            pltpu.SMEM((prompts, 128), jnp.int32),
            pltpu.SMEM((prompts,), jnp.int32),
            pltpu.SMEM((8,), jnp.int32),
        ],
        compiler_params=pltpu.CompilerParams(vmem_limit_bytes=56 * MIB),
        name="prefix_attention",
    )(rollout_task_map.reshape(-1), slot_block_table, qall.reshape(rows_all, WIDTH), prefix_key_value_pool)

    hidden, values = pl.pallas_call(
        finish_entry,
        out_shape=(sds((ROWS, CHUNK), BF16), sds((4, 16), F32)),
        in_specs=[vmem, vmem, vmem, vmem, vmem, anyw, vmem, vmem, vmem, vmem],
        out_specs=(vmem, vmem),
        scratch_shapes=[
            pltpu.VMEM((WIDTH, MODEL_WIDTH), BF16),
            pltpu.VMEM((NZ, ROWS, WIDTH), BF16),
            pltpu.VMEM((NZ, 8, HEAD), F32),
            pltpu.VMEM((ROWS, WIDTH), F32),
            pltpu.VMEM((ROWS, CHUNK), F32),
            pltpu.VMEM((2, NY // 2, NZ, ROWS, WIDTH), BF16),
            pltpu.VMEM((2, NZ // 2, NY, ROWS, WIDTH), BF16),
            pltpu.VMEM((2, NY // 2, NZ, 8, HEAD), F32),
            pltpu.VMEM((2, NZ // 2, NY, 8, HEAD), F32),
            pltpu.VMEM((2, NZ // 2, 1, ROWS, WIDTH), BF16),
            pltpu.VMEM((2, NZ // 2, 8, HEAD), F32),
            pltpu.VMEM((NH, ROWS, CHUNK), BF16),
            pltpu.VMEM((NH - 1, ROWS, CHUNK), BF16),
            pltpu.VMEM((8, HEAD), F32),
            pltpu.VMEM((NH - 1, 8, HEAD), F32),
            dma(()),
            dma((2, NZ // 2, NZ)),
            dma((2, NZ // 2, NZ)),
            dma((2, NZ // 2)),
            dma((2, NZ // 2)),
            dma((2, NZ // 2, 1)),
            dma((2, NZ // 2, 1)),
            dma((2, NZ // 2)),
            dma((2, NZ // 2)),
            dma((NH - 1,)),
            dma((NH - 1,)),
            dma((NH - 1,)),
            dma((NH - 1,)),
        ],
        compiler_params=pltpu.CompilerParams(
            collective_id=1, has_side_effects=True, vmem_limit_bytes=48 * MIB
        ),
        name="reduce_and_project",
    )(
        o.reshape(NY, NZ, ROWS, WIDTH), l.reshape(NY, NZ, 8, HEAD), oloc, lloc,
        residual.reshape(ROWS, CHUNK), output_projection_weight, adapter_down_weight,
        adapter_up_weight, post_norm_gain.reshape(1, CHUNK), value_head_weight.reshape(1, CHUNK),
    )
    return hidden.reshape(residual.shape), values


def prefix_kernel_entry(rc, *refs):
    prefix_kernel(rc, *refs, 64)


def solution(mesh):
    placed = (
        P("seq", None, "head"),
        P(None, "seq", None, "head"),
        P(None, "seq", None, "head"),
        P(None, "seq", None, "head"),
        P("seq", None, "head"),
        P("seq"),
        P(),
        P("seq"),
        P("head", None),
        P("head", None),
        P(),
        P("head"),
        P("head"),
    )
    return jax.shard_map(
        local,
        mesh=mesh,
        in_specs=placed,
        out_specs=(P("seq", None, "head"), P("seq", None)),
        check_vma=False,
    )
```

time: 538 us -> 130 us (0.24)
  blocking collectives: 193 us -> 0 us
  waiting for transfers between devices: 131 us -> 0 us
  Pallas kernels: 0 us -> 118 us
  local copies, waits for them, and re-layouts: 79.7 us -> 10.9 us
  other arithmetic: 56.9 us -> 0 us
  matrix products: 48.2 us -> 0 us
  between operations: 14 us -> 0.74 us
  loops' own time: 11.3 us -> 0 us
    psum x3 -> x0, blocking collectives: 193 us -> none  [the longest x1 165 us: local(): summed_out, summed_sum = lax.psum((prefix_out, prefix_sum), 'seq')]
    pallas_call x0 -> x3, Pallas kernels: none -> 118 us  [the longest x1 55.9 us: local(): pl.pallas_call(finish_entry, out_shape=(sds((ROWS, CHUNK), BF16), sds((4,...]
    all_gather x1 -> x0, waiting for transfers between devices: 69.7 us -> none  [local(): gathered = lax.all_gather(queries, 'seq', axis=0, tiled=True)]
    scatter-add x14 -> x0, other arithmetic: 48.4 us -> none  [the longest x7 35.6 us: prompt_block(): running_out.at[member_rows]]
    dot_general x23 -> x0, matrix products: 48.2 us -> none  [the longest x10 23.1 us: block_terms(): jnp.einsum('mgqk,kgh->mgqh', weights.astype(jnp.bfloat16), block_values,...]
    unnamed x4 -> x0, waiting for transfers between devices: 34.6 us -> none
    psum x1 -> x0, waiting for transfers between devices: 27.2 us -> none  [local(): summed_out, summed_sum = lax.psum((prefix_out, prefix_sum), 'seq')]
    gather x7 -> x0, local copies, waits for them, and re-layouts: 20 us -> none  [prompt_block(): picked = all_queries[jnp.minimum(member_rows, rollouts - 1)]]
  transfers between devices with their start and end apart: 3 -> 0, of which waited for: 3 -> 0; matrix products, arithmetic and copies ran while one was open for 6% -> 0% of each run, Pallas kernels for 0% -> 0%
where the time goes in v1:
time: 130 us
  Pallas kernels  118 us (91%)
  local copies, waits for them, and re-layouts  10.9 us (8%)
    pallas_call x1, Pallas kernels, local(): pl.pallas_call(finish_entry, out_shape=(sds((ROWS, CHUNK), BF16), sds((4,...  55.9 us
    pallas_call x1, Pallas kernels, local(): pl.pallas_call(functools.partial(prefix_kernel_entry, rc), out_shape=(sds...  33.4 us
    pallas_call x1, Pallas kernels, local(): pl.pallas_call(gather_kernel, out_shape=(sds((NY, NZ, ROWS, WIDTH), BF16)...  29 us
    unnamed x27, local copies, waits for them, and re-layouts  10.9 us

profile of v1, /device:TPU:1, one launch (start us, length us, event | category | flops | bytes accessed | tf_op | source)
XLA Modules:
  0.0 129.9 jit_solution(12721921139849374484)
XLA Ops:
  0.6 0.0 copy-start
  0.6 3.4 %copy-done = bf16[2,4,2048,256]{3,2,1,0:T(8,128)(2,1)S(1)} copy-done((bf16[2,4,2048,256]{3,2,1,0:T(8,128)(2,1)S(1)}, bf16[2,4,2048,256]{3,2,1,0:T(8,128)(2,1)}, u32[]{:S(2)}) %copy-start) | copy-done | bytes 8388632
  4.0 0.0 copy-start.6
  4.0 0.8 copy-done.6
  4.9 0.0 copy-start.7
  4.9 0.8 copy-done.7
  5.7 0.7 copy-done.8
  6.3 29.0 %gather_queries.1 = (bf16[4,8,64,512]{3,2,1,0:T(8,128)(2,1)S(1)}, f32[64,512]{1,0:T(8,128)S(1)}, f32[64,512]{1,0:T(8,128)S(1)}) custom-call(s32[4]{0:T(128)S(1)} %copy-done.8, bf16[64,512]{1,0:T(8,128)(2,1)S(1)} %bitcast.12, bf16[2,4,16,256]{3,2,1,0:T(8,128)(2,1)S(1)} %copy-done.7, bf16[2,4,2048,256]{3,2,1,0:T(8,128)(2,1)S(1)} %copy-done), custom_call_target="tpu_custom_call" | custom-call | tf_op jit(solution)/shard_map/gather_queries/pallas_call | solution.py:584
  35.4 0.0 copy-start.2
  35.4 1.3 %copy-done.2 = bf16[4,8,64,512]{3,2,1,0:T(8,128)(2,1)} copy-done((bf16[4,8,64,512]{3,2,1,0:T(8,128)(2,1)}, bf16[4,8,64,512]{3,2,1,0:T(8,128)(2,1)S(1)}, u32[]{:S(2)}) %copy-start.2) | copy-done | bytes 2097176
  36.7 0.0 copy-start.5
  36.7 33.4 %prefix_attention.1 = (bf16[2048,512]{1,0:T(8,128)(2,1)}, f32[32,8,128]{2,1,0:T(8,128)}) custom-call(s32[128]{0:T(128)} %bitcast.13, s32[8]{0:T(128)} %refs_1_.1, bf16[2048,512]{1,0:T(8,128)(2,1)} %bitcast.8, bf16[2,8,512,256]{3,2,1,0:T(8,128)(2,1)} %refs_3_.1), custom_call_target="tpu_custom_call" | custom-call | tf_op jit(solution)/shard_map/prefix_attention/pallas_call | solution.py:609
  70.1 0.0 copy-done.9
  70.1 0.1 copy.15.refs_6_
  70.2 0.0 copy-done.10
  70.2 0.0 copy-done.11
  70.2 0.0 copy-done.3
  70.3 0.0 copy-done.5
  70.3 0.0 copy-start.1
  70.3 1.6 %copy-done.1 = bf16[2048,512]{1,0:T(8,128)(2,1)S(1)} copy-done((bf16[2048,512]{1,0:T(8,128)(2,1)S(1)}, bf16[2048,512]{1,0:T(8,128)(2,1)}, u32[]{:S(2)}) %copy-start.1) | copy-done | bytes 2097176
  71.9 0.9 copy-done.4
  72.8 55.9 %reduce_and_project.1 = (bf16[64,576]{1,0:T(8,128)(2,1)S(1)}, f32[4,16]{1,0:T(4,128)S(1)}) custom-call(bf16[4,8,64,512]{3,2,1,0:T(8,128)(2,1)S(1)} %bitcast.7, f32[4,8,8,128]{3,2,1,0:T(8,128)S(1)} %bitcast.9, f32[64,512]{1,0:T(8,128)S(1)} %get-tuple-element.12.refs_2_, f32[64,512]{1,0:T(8,128)S(1)} %get-tuple-element.13.refs_3_, ...), custom_call_target="tpu_custom_call" | custom-call | tf_op jit(solution)/shard_map/reduce_and_project/pallas_call | solution.py:629
  128.6 0.6 copy.18
  129.3 0.6 copy.19
  (8 shorter events, 0.0 us)
Async XLA Ops:
  0.6 3.4 %copy-start = (bf16[2,4,2048,256]{3,2,1,0:T(8,128)(2,1)S(1)}, bf16[2,4,2048,256]{3,2,1,0:T(8,128)(2,1)}, u32[]{:S(2)}) copy-start(bf16[2,4,2048,256]{3,2,1,0:T(8,128)(2,1)} %resp_ref.1) | copy-start | bytes 25165828
  4.0 0.8 copy-start.6
  4.9 0.8 copy-start.7
  5.7 0.7 copy-start.8
  35.4 1.3 %copy-start.2 = (bf16[4,8,64,512]{3,2,1,0:T(8,128)(2,1)}, bf16[4,8,64,512]{3,2,1,0:T(8,128)(2,1)S(1)}, u32[]{:S(2)}) copy-start(bf16[4,8,64,512]{3,2,1,0:T(8,128)(2,1)S(1)} %get-tuple-element.9) | copy-start | bytes 6291460
  36.7 33.4 %copy-start.9 = (bf16[512,16]{0,1:T(8,128)(2,1)S(1)}, bf16[512,16]{0,1:T(8,128)(2,1)}, u32[]{:S(2)}) copy-start(bf16[512,16]{0,1:T(8,128)(2,1)} %param.22) | copy-start | bytes 49156
  36.7 33.5 %copy-start.10 = (f32[576]{0:T(1024)S(1)}, f32[576]{0:T(1024)}, u32[]{:S(2)}) copy-start(f32[576]{0:T(1024)} %param.24) | copy-start | bytes 6916
  36.7 33.5 %copy-start.11 = (f32[576]{0:T(1024)S(1)}, f32[576]{0:T(1024)}, u32[]{:S(2)}) copy-start(f32[576]{0:T(1024)} %param.25) | copy-start | bytes 6916
  36.7 33.6 %copy-start.3 = (bf16[16,4608]{1,0:T(8,128)(2,1)S(1)}, bf16[16,4608]{1,0:T(8,128)(2,1)}, u32[]{:S(2)}) copy-start(bf16[16,4608]{1,0:T(8,128)(2,1)} %refs_7_.1) | copy-start | bytes 442372
  36.7 33.6 %copy-start.5 = (bf16[4,16,576]{2,1,0:T(8,128)(2,1)S(1)}, bf16[4,16,576]{2,1,0:T(8,128)(2,1)}, u32[]{:S(2)}) copy-start(bf16[4,16,576]{2,1,0:T(8,128)(2,1)} %param.17) | copy-start | bytes 221188
  70.3 1.6 %copy-start.1 = (bf16[2048,512]{1,0:T(8,128)(2,1)S(1)}, bf16[2048,512]{1,0:T(8,128)(2,1)}, u32[]{:S(2)}) copy-start(bf16[2048,512]{1,0:T(8,128)(2,1)} %get-tuple-element.10) | copy-start | bytes 6291460
  71.9 0.9 copy-start.4

commit v2 on v1

v2 whole, which is shorter than its diff:
```python
import functools

import jax
import jax.numpy as jnp
from jax import lax
from jax.experimental import pallas as pl
from jax.experimental.pallas import tpu as pltpu
from jax.sharding import PartitionSpec as P

MODEL_WIDTH = 4608
HEAD = 128
SYS_BLOCKS = 64
PROMPT_BLOCKS = 16
EPS = 1e-06
C1 = 144.0 ** (-0.5) / 50.0
C2 = 50.0 * 1.4426950408889634

NY, NZ, NH = 4, 8, 8
ROWS = 64
WIDTH = 512
HEADS = 4
CHUNK = 576
GROUP = 12
PADDED = 640
MIB = 1 << 20
K1_MIB, K2_MIB, K3_MIB = 58, 58, 58
MESH = pl.DeviceIdType.MESH
F32 = jnp.float32
BF16 = jnp.bfloat16


def weight_of(scores):
    return jnp.exp2(jnp.tanh(scores * C1) * C2)


def dot_t(a, b):
    return lax.dot_general(a, b, (((1,), (1,)), ((), ())), preferred_element_type=F32)


def dot(a, b):
    return jnp.dot(a, b, preferred_element_type=F32)


def lane_sum(p):
    total = p[:, :HEAD]
    for i in range(1, p.shape[1] // HEAD):
        total = total + p[:, i * HEAD : (i + 1) * HEAD]
    return total


def position():
    seq = lax.axis_index("seq")
    head = lax.axis_index("head")
    return lax.div(seq, NZ), lax.rem(seq, NZ), head


def wrap(v, n):
    return lax.rem(v + 2 * n, n)


def shifted(y, z, head, axis, step):
    if axis == 0:
        return (wrap(y + step, NY) * NZ + z, head)
    return (y * NZ + wrap(z + step, NZ), head)


def cols(h):
    return slice(h * HEAD, (h + 1) * HEAD)


def chosen(slot_ref, sys_blocks, ranks):
    found = [jnp.int32(0) for _ in ranks]
    seen = jnp.int32(0)
    for i in range(slot_ref.shape[0]):
        is_sys = (slot_ref[i] < sys_blocks).astype(jnp.int32)
        for n, rank in enumerate(ranks):
            found[n] = found[n] + i * is_sys * (seen == rank).astype(jnp.int32)
        seen = seen + is_sys
    return [(f, jnp.where(seen > rank, 1.0, 0.0)) for f, rank in zip(found, ranks)]


def head_picker():
    lane = lax.broadcasted_iota(jnp.int32, (8, WIDTH), 1)
    row = lax.broadcasted_iota(jnp.int32, (8, WIDTH), 0)
    return jnp.where(lax.div(lane, HEAD) == row, 1.0, 0.0).astype(BF16)


def head_sums(picker, lanes):
    hi = lanes.astype(BF16)
    lo = (lanes - hi.astype(F32)).astype(BF16)
    return dot_t(picker, hi) + dot_t(picker, lo)


def system_round(load_q, store, pool, picks, qtmp, sbuf, otmp, lbuf, arrived=None):
    for m in range(8):
        qtmp[m * ROWS : (m + 1) * ROWS, :] = load_q(m)
    (b0, v0), (b1, v1) = picks

    def score(h, b):
        return dot_t(qtmp[:, cols(h)], pool[0, b, :, cols(h // 2)])

    sbuf[0] = score(0, b0)
    for h in range(HEADS):
        g = h // 2
        sbuf[1] = score(h, b1)
        p0 = weight_of(sbuf[0])
        l0 = lane_sum(p0)
        o0 = dot(p0.astype(BF16), pool[1, b0, :, cols(g)])
        if h < HEADS - 1:
            sbuf[0] = score(h + 1, b0)
        p1 = weight_of(sbuf[1])
        l1 = lane_sum(p1)
        o1 = dot(p1.astype(BF16), pool[1, b1, :, cols(g)])
        otmp[:, cols(h)] = o0 * v0 + o1 * v1
        lbuf[:, cols(h)] = l0 * v0 + l1 * v1
    total = head_sums(head_picker(), lbuf[...])
    if arrived is not None:
        arrived()
    for m in range(8):
        at = slice(m * ROWS, (m + 1) * ROWS)
        store(m, otmp[at, :], total[:, at])


def gather_kernel(
    len_ref, slot_ref, q_ref, inc_ref, map_ref, resp_ref, pool_ref,
    qall, acc_out, sums, oloc, lloc, table,
    cache, pool, acc, qtmp, sbuf, otmp, lbuf, load_sem, pool_sem, acc_sem, s1, r1, s2, r2,
):
    y, z, head = position()
    core = lax.rem(head, 2)

    barrier = pltpu.get_barrier_semaphore()
    for axis in (0, 1):
        for step in (1, -1):
            pl.semaphore_signal(
                barrier, inc=1, device_id=shifted(y, z, head, axis, step), device_id_type=MESH
            )
    loads = []
    for i in range(4):
        c = pltpu.make_async_copy(resp_ref.at[:, i], cache.at[i], load_sem.at[i])
        c.start()
        loads.append(c)
    pool_load = pltpu.make_async_copy(pool_ref, pool, pool_sem)
    pool_load.start()
    qall[y, z] = q_ref[...]
    picks = chosen(slot_ref, SYS_BLOCKS, (0, 1))
    pl.semaphore_wait(barrier, 4)

    def list_members():
        task = jnp.broadcast_to(map_ref[...].astype(F32), (HEAD, HEAD))
        across = jnp.transpose(task)
        row = lax.broadcasted_iota(jnp.int32, (HEAD, HEAD), 0)
        lane = lax.broadcasted_iota(jnp.int32, (HEAD, HEAD), 1)
        earlier = jnp.where((task == across) & (lane < row), 1.0, 0.0)
        rank = jnp.sum(earlier, axis=1, keepdims=True)
        spot = jnp.where(rank == lane.astype(F32), 1.0, 0.0).astype(BF16)
        mine = across[:16] == row[:16].astype(F32)
        ids = jnp.where(mine, lane[:16].astype(F32), 0.0).astype(BF16)
        count = jnp.sum(jnp.where(mine, 1.0, 0.0), axis=1, keepdims=True)
        table[...] = jnp.where(lane[:16] == HEAD - 1, count, dot(ids, spot)).astype(jnp.int32)

    def attend(i):
        loads[i].wait()
        length = len_ref[i]
        rows = slice(i * 16, (i + 1) * 16)

        def group(g, _):
            def at(j):
                return pl.ds(pl.multiple_of((2 * g + j) * HEAD, HEAD), HEAD)

            gc = pl.ds(pl.multiple_of(g * HEAD, HEAD), HEAD)
            lhs = jnp.concatenate([q_ref[rows, at(0)], q_ref[rows, at(1)]], axis=0)
            out = jnp.zeros((32, HEAD), F32)
            total = jnp.zeros((32, HEAD), F32)
            for part in range(4):
                keys = slice(part * 512, (part + 1) * 512)
                p = weight_of(dot_t(lhs, cache[i, 0, keys, gc]))
                where = lax.broadcasted_iota(jnp.int32, p.shape, 1) + part * 512
                p = jnp.where(where < length, p, 0.0)
                total = total + lane_sum(p)
                out = out + dot(p.astype(BF16), cache[i, 1, keys, gc])
            p = weight_of(dot_t(lhs, inc_ref[0, i, :, gc]))
            n = lax.rem(lax.broadcasted_iota(jnp.int32, p.shape, 0), 16)
            m = lax.broadcasted_iota(jnp.int32, p.shape, 1)
            p = jnp.where(m <= n, p, 0.0)
            out = out + dot(p.astype(BF16), inc_ref[1, i, :, gc])
            wide = jnp.broadcast_to(
                jnp.sum(total, axis=1, keepdims=True) + jnp.sum(p, axis=1, keepdims=True), (32, HEAD)
            )
            for j in range(2):
                oloc[rows, at(j)] = out[j * 16 : (j + 1) * 16]
                lloc[rows, at(j)] = wide[j * 16 : (j + 1) * 16]
            return 0

        lax.fori_loop(0, 2, group, 0)

    def copies(axis1):
        axis2 = 1 - axis1
        n1, n2 = (NY, NZ) if axis1 == 0 else (NZ, NY)
        c1, c2 = (y, z) if axis1 == 0 else (z, y)
        h1, h2 = n1 // 2, n2 // 2
        offsets = [0]
        for k in range(1, h1):
            offsets += [-k, k]
        offsets.append(h1)

        def piece(i1, i2, part):
            a, b = (i1, i2) if axis1 == 0 else (i2, i1)
            view = qall.at[a, b]
            return view if part is None else view.at[pl.ds(part * (ROWS // 2), ROWS // 2)]

        def first(d, k):
            s = 1 - 2 * d
            view = piece(wrap(c1 - s * k, n1), c2, d if k == h1 - 1 else None)
            return pltpu.make_async_remote_copy(
                src_ref=view, dst_ref=view, send_sem=s1.at[d, k], recv_sem=r1.at[d, k],
                device_id=shifted(y, z, head, axis1, s), device_id_type=MESH,
            )

        def second(j, d, k):
            s = 1 - 2 * d
            view = piece(wrap(c1 + offsets[j], n1), wrap(c2 - s * k, n2), d if k == h2 - 1 else None)
            return pltpu.make_async_remote_copy(
                src_ref=view, dst_ref=view, send_sem=s2.at[d, j, k], recv_sem=r2.at[d, j, k],
                device_id=shifted(y, z, head, axis2, s), device_id_type=MESH,
            )

        def phase1(work):
            for d in (0, 1):
                first(d, 0).start()
            for d in (0, 1):
                second(0, d, 0).start()
            for k in range(h1):
                for i in work[k]:
                    attend(i)
                for d in (0, 1):
                    first(d, k).wait_recv()
                    if k < h1 - 1:
                        first(d, k + 1).start()
                if k < h1 - 1:
                    for d in (0, 1):
                        for e in (0, 1):
                            second(1 + 2 * k + d, e, 0).start()
                else:
                    for e in (0, 1):
                        second(n1 - 1, e, 0).start()

        def forward(k):
            for j in range(n1):
                for d in (0, 1):
                    second(j, d, k).wait_recv()
                    if k < h2 - 1:
                        second(j, d, k + 1).start()

        def drain():
            for k in range(h1):
                for d in (0, 1):
                    first(d, k).wait_send()
            for k in range(h2):
                for j in range(n1):
                    for d in (0, 1):
                        second(j, d, k).wait_send()

        return phase1, forward, drain

    def on(core_index, action):
        @pl.when(core == core_index)
        def _():
            action()

    def start0():
        phase1, forward, _ = copies(0)
        phase1(([0], [1]))
        attend(2)
        attend(3)
        list_members()
        forward(0)

    def start1():
        copies(1)[0](([0], [1], [2], [3]))
        list_members()

    on(0, start0)
    on(1, start1)
    pool_load.wait()

    def keep(at):
        return pltpu.make_async_copy(acc.at[at], acc_out.at[at], acc_sem.at[at])

    def compute(pair, y_step):
        def coords(m):
            a = wrap(z + pair[m // 4], NZ)
            return (
                jnp.where(core == 0, m % 4, wrap(y + y_step, NY)),
                jnp.where(core == 0, a, m),
            )

        def load_q(m):
            return qall[coords(m)]

        def store(m, out, total):
            at = coords(m)
            acc[at] = out
            keep(at).start()
            sums[at] = jnp.concatenate([total, jnp.zeros((8, HEAD - ROWS), F32)], axis=1)

        system_round(load_q, store, pool, picks, qtmp, sbuf, otmp, lbuf)

    def in_round(r, index, core_index, action):
        @pl.when((r == index) & (core == core_index))
        def _():
            action()

    def one_round(r, _):
        compute((r, -1 - r), jnp.where(r == 1, -1, jnp.where(r == 2, 1, jnp.where(r == 3, 2, 0))))
        for k in range(3):
            in_round(r, k, 0, lambda: copies(0)[1](k + 1))
        in_round(r, 0, 1, lambda: copies(1)[1](0))
        in_round(r, 2, 1, lambda: copies(1)[1](1))
        return 0

    lax.fori_loop(0, 4, one_round, 0)
    on(0, lambda: copies(0)[2]())
    on(1, lambda: copies(1)[2]())
    for a in range(NY):
        for b in range(NZ):
            keep((a, b)).wait()


def prefix_kernel(
    rc, slot_ref, table_ref, q_ref, pool_hbm, lin_ref, acc_out, l_ref, sel,
    pool_ref, acc, lanes, sbuf, qbuf, obuf, lbuf, system, item_slot, item_prompt, item_part, pool_sem, acc_sem,
):
    pool_load = pltpu.make_async_copy(pool_hbm, pool_ref, pool_sem)
    pool_load.start()
    slots = slot_ref.shape[0]
    total_rows = q_ref.shape[0]
    chunks = total_rows // rc

    for i in range(8):
        system[i] = 0
    count = jnp.int32(0)
    items_p = jnp.int32(0)
    for i in range(slots):
        logical = slot_ref[i]
        system[count] = i
        count = count + (logical < SYS_BLOCKS).astype(jnp.int32)
        p = lax.div(jnp.maximum(logical - SYS_BLOCKS, 0), PROMPT_BLOCKS)
        n = jnp.where(logical < SYS_BLOCKS, 0, table_ref[p, HEAD - 1])
        for c in range(2):
            item_slot[items_p] = i
            item_prompt[items_p] = p
            item_part[items_p] = c
            items_p = items_p + (n > c * GROUP).astype(jnp.int32)
    count = jnp.maximum(count - 4, 0)

    def rows_of(c):
        return pl.ds(pl.multiple_of(c * rc, rc), rc)

    def score(item, h):
        c = lax.div(item, count)
        b = system[4 + lax.rem(item, count)]
        return dot_t(q_ref[rows_of(c), cols(h)], pool_ref[0, b, :, cols(h // 2)])

    acc[...] = jnp.zeros_like(acc)
    lanes[...] = jnp.zeros_like(lanes)
    pool_load.wait()
    for n in range(2):
        for kv in range(2):
            sel[kv, n] = pool_ref[kv, system[2 + n]]

    @pl.when(count > 0)
    def _():
        items = count * chunks
        sbuf[0] = score(0, 0)

        def step(item, _):
            rows = rows_of(lax.div(item, count))
            turn = lax.rem(item, count)
            b = system[4 + turn]
            following = jnp.minimum(item + 1, items - 1)
            for h in range(HEADS):
                if h < HEADS - 1:
                    sbuf[(h + 1) % 2] = score(item, h + 1)
                else:
                    sbuf[0] = score(following, 0)
                p = weight_of(sbuf[h % 2])
                part = lane_sum(p)
                out = dot(p.astype(BF16), pool_ref[1, b, :, cols(h // 2)])
                lanes[rows, cols(h)] += part
                acc[rows, cols(h)] += out
            return 0

        lax.fori_loop(0, items, step, 0)

    rows_g = GROUP * 16

    def pick(k, turn):
        p = item_prompt[k]
        c = item_part[k]
        for m in range(GROUP):
            r = table_ref[p, c * GROUP + m]
            qbuf[turn, m * 16 : (m + 1) * 16, :] = q_ref[pl.ds(pl.multiple_of(r * 16, 16), 16), :]

    def member_score(k, turn, g):
        lhs = jnp.concatenate([qbuf[turn, :, cols(2 * g)], qbuf[turn, :, cols(2 * g + 1)]], axis=0)
        return dot_t(lhs, pool_ref[0, item_slot[k], :, cols(g)])

    def member_weights(k, g):
        w = weight_of(sbuf[g, : 2 * rows_g])
        part = lane_sum(w)
        out = dot(w.astype(BF16), pool_ref[1, item_slot[k], :, cols(g)])
        for j in range(2):
            at = slice(j * rows_g, (j + 1) * rows_g)
            obuf[:, cols(2 * g + j)] = out[at]
            lbuf[:, cols(2 * g + j)] = part[at]

    @pl.when(items_p > 0)
    def _():
        pick(0, 0)
        sbuf[0, : 2 * rows_g] = member_score(0, 0, 0)

        def one(k, _):
            turn = lax.rem(k, 2)
            following = jnp.minimum(k + 1, items_p - 1)
            sbuf[1, : 2 * rows_g] = member_score(k, turn, 1)
            pick(following, 1 - turn)
            member_weights(k, 0)
            sbuf[0, : 2 * rows_g] = member_score(following, 1 - turn, 0)
            member_weights(k, 1)
            p = item_prompt[k]
            c = item_part[k]
            n = table_ref[p, HEAD - 1]
            for m in range(GROUP):
                r = table_ref[p, c * GROUP + m]
                at = pl.ds(pl.multiple_of(r * 16, 16), 16)
                src = slice(m * 16, (m + 1) * 16)
                there = jnp.where(c * GROUP + m < n, 1.0, 0.0)
                acc[at, :] += obuf[src, :] * there
                lanes[at, :] += lbuf[src, :] * there
            return 0

        lax.fori_loop(0, items_p, one, 0)

    acc_store = pltpu.make_async_copy(acc, acc_out, acc_sem)
    acc_store.start()
    picker = head_picker()

    def finish(c, _):
        total = head_sums(picker, lanes[pl.ds(pl.multiple_of(c * 512, 512), 512), :])
        for m in range(8):
            l_ref[c * 8 + m] = lin_ref[c * 8 + m]
            l_ref[c * 8 + m, :, :ROWS] += total[:, m * ROWS : (m + 1) * ROWS]
        return 0

    lax.fori_loop(0, total_rows // 512, finish, 0)
    acc_store.wait()


def finish_kernel(
    slot_ref, l_ref, q_ref, oloc, lloc, res_ref, pool, first_ref, second_ref, w_ref, down_ref, up_ref, gain_ref, vhw_ref,
    hid_ref, val_ref,
    wbuf, acc, acc2, sums, far, qtmp, sbuf, otmp, lbuf, part1, lpart1, mine, pmine,
    rb_y, rb_z, rl_y, rl_z, rb2, rl2, chunk, rchunk, small, rsmall,
    w_sem, a_sem, s1, r1, t1, u1, s2, r2, t2, u2, hs, hr, ss, sr,
):
    y, z, head = position()
    core = lax.rem(head, 2)
    seq = y * NZ + z
    barrier = pltpu.get_barrier_semaphore()

    def on(core_index, action):
        @pl.when(core == core_index)
        def _():
            action()

    def greet(to):
        pl.semaphore_signal(barrier, inc=1, device_id=to, device_id_type=MESH)

    def greet_axes(ring, direct, n):
        for step in (1, -1):
            greet(shifted(y, z, head, ring, step))
        for t in range(1, n):
            greet(shifted(y, z, head, direct, t))

    for t in range(1, NH):
        greet((seq, wrap(head + t, NH)))
    on(0, lambda: greet_axes(1, 0, NY))
    on(1, lambda: greet_axes(0, 1, NZ))
    parts = [
        pltpu.make_async_copy(first_ref, acc, a_sem.at[0]),
        pltpu.make_async_copy(second_ref, acc2, a_sem.at[1]),
    ]
    for x in parts:
        x.start()
    wcopy = pltpu.make_async_copy(w_ref, wbuf, w_sem)
    wcopy.start()
    picks = [(n, v) for n, (_, v) in enumerate(chosen(slot_ref, SYS_BLOCKS, (2, 3)))]

    def compute(pair, y_step, arrived):
        def coords(m):
            a = wrap(z + pair[m // 4], NZ)
            return (
                jnp.where(core == 0, m % 4, wrap(y + y_step, NY)),
                jnp.where(core == 0, a, m),
            )

        def load_q(m):
            return q_ref[coords(m)]

        def store(m, out, total):
            at = coords(m)
            acc[at] = (acc[at] + acc2[at]) + out
            sums[at] = l_ref[at] + jnp.concatenate([total, jnp.zeros((8, HEAD - ROWS), F32)], axis=1)

        system_round(load_q, store, pool, picks, qtmp, sbuf, otmp, lbuf, arrived)

    half = ROWS // 2

    def ring(axis1):
        axis2 = 1 - axis1
        n1, n2 = (NY, NZ) if axis1 == 0 else (NZ, NY)
        c1, c2 = (y, z) if axis1 == 0 else (z, y)
        h = n1 // 2
        rb, rl = (rb_y, rl_y) if axis1 == 0 else (rb_z, rl_z)
        order = [wrap(c2 + t, n2) for t in list(range(n2 // 2, n2)) + list(range(0, n2 // 2))]

        def own(i, j):
            return acc[i, j] if axis1 == 0 else acc[j, i]

        def own_l(i):
            return sums.at[i] if axis1 == 0 else sums.at[:, i]

        def copy(d, k, j):
            if k == 0:
                src = far.at[j, pl.ds(d * half, half)]
                dst = rb.at[d, 0, j, pl.ds(d * half, half)]
            else:
                src = rb.at[d, k - 1, j]
                dst = rb.at[d, k, j]
            return pltpu.make_async_remote_copy(
                src_ref=src, dst_ref=dst, send_sem=s1.at[d, k, j], recv_sem=r1.at[d, k, j],
                device_id=shifted(y, z, head, axis1, 1 - 2 * d), device_id_type=MESH,
            )

        def copy_l(d, k):
            s = 1 - 2 * d
            src = own_l(wrap(c1 + s * (h - k), n1)) if k == d else rl.at[d, k - 1]
            return pltpu.make_async_remote_copy(
                src_ref=src, dst_ref=rl.at[d, k], send_sem=t1.at[d, k], recv_sem=u1.at[d, k],
                device_id=shifted(y, z, head, axis1, s), device_id_type=MESH,
            )

        def begin():
            for j in order:
                far[j] = own(wrap(c1 + h, n1), j).astype(BF16)
                for d in (0, 1):
                    copy(d, 0, j).start()
            copy_l(0, 0).start()

        def step(d, k):
            to = wrap(c1 + (1 - 2 * d) * (h - k), n1)
            for j in order:
                copy(d, k - 1, j).wait_recv()
                here = own(to, j)
                if k == 1:
                    a = pl.ds(d * half, half)
                    b = pl.ds((1 - d) * half, half)
                    there = rb[d, 0, j, a].astype(F32)
                    rb[d, 0, j, a] = (there + here[d * half : (d + 1) * half]).astype(BF16)
                    rb[d, 0, j, b] = here[(1 - d) * half : (2 - d) * half].astype(BF16)
                else:
                    rb[d, k - 1, j] = (rb[d, k - 1, j].astype(F32) + here).astype(BF16)
                copy(d, k, j).start()
            if k > d:
                copy_l(d, k - 1).wait_recv()
                rl[d, k - 1] = rl[d, k - 1] + own_l(to)[...]
            copy_l(d, k).start()

        def direct(t):
            return pltpu.make_async_remote_copy(
                src_ref=part1.at[t], dst_ref=rb2.at[t], send_sem=s2.at[t], recv_sem=r2.at[t],
                device_id=shifted(y, z, head, axis2, t), device_id_type=MESH,
            )

        def direct_l(t):
            return pltpu.make_async_remote_copy(
                src_ref=lpart1.at[t], dst_ref=rl2.at[t], send_sem=t2.at[t], recv_sem=u2.at[t],
                device_id=shifted(y, z, head, axis2, t), device_id_type=MESH,
            )

        def final():
            turns = sorted(range(1, n2), key=lambda t: -min(t, n2 - t)) + [0]
            for n, t in enumerate(turns):
                j = wrap(c2 + t, n2)
                for d in (0, 1):
                    copy(d, h - 1, j).wait_recv()
                v = own(c1, j) + rb[0, h - 1, j].astype(F32) + rb[1, h - 1, j].astype(F32)
                if t == 0:
                    mine[...] = v
                else:
                    part1[t] = v.astype(BF16)
                    direct(t).start()
            for d in (0, 1):
                copy_l(d, h - 1).wait_recv()
            for t in turns:
                j = wrap(c2 + t, n2)
                at = (c1, j) if axis1 == 0 else (j, c1)
                v = sums[at] + rl[0, h - 1, j] + rl[1, h - 1, j]
                if t == 0:
                    small[...] = v
                else:
                    lpart1[t] = v
                    direct_l(t).start()
            v = mine[...]
            w = small[...]
            for t in turns[:-1]:
                direct(t).wait_recv()
                v = v + rb2[t].astype(F32)
            for t in turns[:-1]:
                direct_l(t).wait_recv()
                w = w + rl2[t]
            mine[...] = v
            small[...] = w
            for d in (0, 1):
                for k in range(h):
                    for j in order:
                        copy(d, k, j).wait_send()
                    if k >= d:
                        copy_l(d, k).wait_send()
            for t in turns[:-1]:
                direct(t).wait_send()
                direct_l(t).wait_send()

        return begin, step, final

    def steps(axis1, pairs):
        step = ring(axis1)[1]
        for d, k in pairs:
            step(d, k)

    def in_round(r, index, core_index, action):
        @pl.when((r == index) & (core == core_index))
        def _():
            action()

    def start(axis1, direct):
        pl.semaphore_wait(barrier, NH - 1 + 2 + direct - 1)
        ring(axis1)[0]()

    def arrived_in(r):
        @pl.when(r == 0)
        def _():
            for x in parts:
                x.wait()

    def one_round(r, _):
        y_step = jnp.where(r == 0, 2, jnp.where(r == 1, 1, jnp.where(r == 2, -1, 0)))
        compute((r - 4, 3 - r), y_step, lambda: arrived_in(r))
        in_round(r, 0, 0, lambda: start(1, NY))
        in_round(r, 0, 1, lambda: start(0, NZ))
        for k in range(1, 4):
            in_round(r, k, 0, lambda: steps(1, ((0, k), (1, k))))
        in_round(r, 1, 1, lambda: steps(0, ((0, 1),)))
        in_round(r, 2, 1, lambda: steps(0, ((1, 1),)))
        return 0

    lax.fori_loop(0, 4, one_round, 0)
    on(0, lambda: ring(1)[2]())
    on(1, lambda: ring(0)[2]())

    sums = jnp.transpose(jnp.concatenate([small[...], jnp.zeros((HEAD - 8, HEAD), F32)], axis=0))
    att = []
    for h in range(HEADS):
        den = sums[:ROWS, h : h + 1] + lloc[:, cols(h)]
        att.append(((mine[:, cols(h)] + oloc[:, cols(h)]) / den).astype(BF16))
    att = jnp.concatenate(att, axis=1)
    low = dot(att, down_ref[...])
    low_hi = low.astype(BF16)
    low_lo = (low - low_hi.astype(F32)).astype(BF16)
    low_lo2 = (low - low_hi.astype(F32) - low_lo.astype(F32)).astype(BF16)
    wcopy.wait()
    sends = {}
    for t in (4, 3, 5, 2, 6, 1, 7, 0):
        to = wrap(head + t, NH)
        odd = lax.rem(to, 2)
        at = pl.ds(pl.multiple_of(to * CHUNK - odd * (HEAD // 2), HEAD), PADDED)
        u = up_ref[:, at]
        v = dot(att, wbuf[:, at]) + (dot(low_hi, u) + dot(low_lo, u) + dot(low_lo2, u))
        v = jnp.where(odd == 1, v[:, HEAD // 2 :], v[:, :CHUNK])
        if t == 0:
            pmine[...] = v
            continue
        chunk[t - 1] = v.astype(BF16)
        x = pltpu.make_async_remote_copy(
            src_ref=chunk.at[t - 1], dst_ref=rchunk.at[t - 1], send_sem=hs.at[t - 1], recv_sem=hr.at[t - 1],
            device_id=(seq, to), device_id_type=MESH,
        )
        x.start()
        sends[t] = x
    p = pmine[...]
    for t in (1, 7, 2, 6, 3, 5, 4):
        sends[t].wait_recv()
        p = p + rchunk[t - 1].astype(F32)

    res = res_ref[...].astype(F32)
    gain = gain_ref[...]
    vhw = vhw_ref[...]
    pg = p * gain
    parts = [p * p, res * res, res * pg, pg * pg, res * vhw, pg * vhw]
    lane = lax.broadcasted_iota(jnp.int32, (ROWS, HEAD), 1)
    packed = jnp.zeros((ROWS, HEAD), F32)
    for i, v in enumerate(parts):
        packed = jnp.where(lane == i, jnp.sum(v, axis=1, keepdims=True), packed)
    packed = jnp.concatenate([packed, jnp.zeros((HEAD - ROWS, HEAD), F32)], axis=0)
    small[...] = jnp.transpose(packed)[:8]
    sends2 = []
    for t in range(1, NH):
        x = pltpu.make_async_remote_copy(
            src_ref=small, dst_ref=rsmall.at[t - 1], send_sem=ss.at[t - 1], recv_sem=sr.at[t - 1],
            device_id=(seq, wrap(head + t, NH)), device_id_type=MESH,
        )
        x.start()
        sends2.append(x)
    total = small[...]
    for t in range(1, NH):
        sends2[t - 1].wait_recv()
        total = total + rsmall[t - 1]
    sq, res2, rpg, pg2, rw, pgw = [total[i : i + 1] for i in range(6)]
    r = lax.rsqrt(sq / MODEL_WIDTH + EPS)
    power = res2 + 2.0 * r * rpg + r * r * pg2
    value = (rw + r * pgw) * lax.rsqrt(power / MODEL_WIDTH + EPS)
    for i in range(4):
        val_ref[i : i + 1, :] = value[:, i * 16 : (i + 1) * 16]
    rcol = jnp.transpose(jnp.broadcast_to(r, (HEAD, HEAD)))[:ROWS, :1]
    hid_ref[...] = (res + pg * rcol).astype(BF16)
    for x in list(sends.values()) + sends2:
        x.wait_send()


def local(
    queries, incoming_key_value, prefix_key_value_pool, response_key_value, residual, lengths,
    rollout_task_map, slot_block_table, output_projection_weight, adapter_down_weight,
    adapter_up_weight, post_norm_gain, value_head_weight,
):
    vmem = pl.BlockSpec(memory_space=pltpu.VMEM)
    smem = pl.BlockSpec(memory_space=pltpu.SMEM)
    hbm = pl.BlockSpec(memory_space=pltpu.HBM)
    dma = pltpu.SemaphoreType.DMA
    sds = jax.ShapeDtypeStruct
    devices = NY * NZ
    rows_all = devices * ROWS
    pool_buf = pltpu.VMEM((2, 8, 512, 256), BF16)
    round_bufs = [
        pltpu.VMEM((8 * ROWS, WIDTH), BF16),
        pltpu.VMEM((2, 512, 512), F32),
        pltpu.VMEM((8 * ROWS, WIDTH), F32),
        pltpu.VMEM((8 * ROWS, WIDTH), F32),
    ]

    qall, acc, sums, oloc, lloc, table = pl.pallas_call(
        gather_kernel,
        out_shape=(
            sds((NY, NZ, ROWS, WIDTH), BF16),
            sds((NY, NZ, ROWS, WIDTH), F32),
            sds((NY, NZ, 8, HEAD), F32),
            sds((ROWS, WIDTH), F32),
            sds((ROWS, WIDTH), F32),
            sds((16, HEAD), jnp.int32),
        ),
        in_specs=[smem, smem, vmem, vmem, vmem, hbm, hbm],
        out_specs=(vmem, hbm, vmem, vmem, vmem, vmem),
        scratch_shapes=[
            pltpu.VMEM((4, 2, 2048, 256), BF16),
            pool_buf,
            pltpu.VMEM((NY, NZ, ROWS, WIDTH), F32),
            *round_bufs,
            dma((4,)),
            dma(()),
            dma((NY, NZ)),
            dma((2, NZ // 2)),
            dma((2, NZ // 2)),
            dma((2, NZ, NZ // 2)),
            dma((2, NZ, NZ // 2)),
        ],
        compiler_params=pltpu.CompilerParams(
            collective_id=0, has_side_effects=True, vmem_limit_bytes=K1_MIB * MIB
        ),
        name="gather_queries",
    )(
        lengths, slot_block_table, queries.reshape(ROWS, WIDTH), incoming_key_value,
        rollout_task_map, response_key_value, prefix_key_value_pool,
    )

    rc = 1024
    acc2, sums2, chosen_blocks = pl.pallas_call(
        functools.partial(prefix_kernel, rc),
        out_shape=(
            sds((rows_all, WIDTH), F32),
            sds((devices, 8, HEAD), F32),
            sds((2, 2, 512, 256), BF16),
        ),
        in_specs=[smem, smem, vmem, hbm, vmem],
        out_specs=(hbm, vmem, vmem),
        scratch_shapes=[
            pool_buf,
            pltpu.VMEM((rows_all, WIDTH), F32),
            pltpu.VMEM((rows_all, WIDTH), F32),
            pltpu.VMEM((2, rc, 512), F32),
            pltpu.VMEM((2, GROUP * 16, WIDTH), BF16),
            pltpu.VMEM((GROUP * 16, WIDTH), F32),
            pltpu.VMEM((GROUP * 16, WIDTH), F32),
            pltpu.SMEM((16,), jnp.int32),
            pltpu.SMEM((24,), jnp.int32),
            pltpu.SMEM((24,), jnp.int32),
            pltpu.SMEM((24,), jnp.int32),
            dma(()),
            dma(()),
        ],
        compiler_params=pltpu.CompilerParams(vmem_limit_bytes=K2_MIB * MIB),
        name="prefix_attention",
    )(
        slot_block_table, table, qall.reshape(rows_all, WIDTH), prefix_key_value_pool,
        sums.reshape(devices, 8, HEAD),
    )

    hidden, values = pl.pallas_call(
        finish_kernel,
        out_shape=(sds((ROWS, CHUNK), BF16), sds((4, 16), F32)),
        in_specs=[smem] + [vmem] * 6 + [hbm] * 3 + [vmem] * 4,
        out_specs=(vmem, vmem),
        scratch_shapes=[
            pltpu.VMEM((WIDTH, MODEL_WIDTH), BF16),
            pltpu.VMEM((NY, NZ, ROWS, WIDTH), F32),
            pltpu.VMEM((NY, NZ, ROWS, WIDTH), F32),
            pltpu.VMEM((NY, NZ, 8, HEAD), F32),
            pltpu.VMEM((NZ, ROWS, WIDTH), BF16),
            *round_bufs,
            pltpu.VMEM((NZ, ROWS, WIDTH), BF16),
            pltpu.VMEM((NZ, 8, HEAD), F32),
            pltpu.VMEM((ROWS, WIDTH), F32),
            pltpu.VMEM((ROWS, CHUNK), F32),
            pltpu.VMEM((2, NY // 2, NZ, ROWS, WIDTH), BF16),
            pltpu.VMEM((2, NZ // 2, NY, ROWS, WIDTH), BF16),
            pltpu.VMEM((2, NY // 2, NZ, 8, HEAD), F32),
            pltpu.VMEM((2, NZ // 2, NY, 8, HEAD), F32),
            pltpu.VMEM((NZ, ROWS, WIDTH), BF16),
            pltpu.VMEM((NZ, 8, HEAD), F32),
            pltpu.VMEM((NH - 1, ROWS, CHUNK), BF16),
            pltpu.VMEM((NH - 1, ROWS, CHUNK), BF16),
            pltpu.VMEM((8, HEAD), F32),
            pltpu.VMEM((NH - 1, 8, HEAD), F32),
            dma(()),
            dma((2,)),
            dma((2, NZ // 2, NZ)),
            dma((2, NZ // 2, NZ)),
            dma((2, NZ // 2)),
            dma((2, NZ // 2)),
            dma((NZ,)),
            dma((NZ,)),
            dma((NZ,)),
            dma((NZ,)),
            dma((NH - 1,)),
            dma((NH - 1,)),
            dma((NH - 1,)),
            dma((NH - 1,)),
        ],
        compiler_params=pltpu.CompilerParams(
            collective_id=1, has_side_effects=True, vmem_limit_bytes=K3_MIB * MIB
        ),
        name="reduce_and_project",
    )(
        slot_block_table, sums2.reshape(NY, NZ, 8, HEAD), qall, oloc, lloc,
        residual.reshape(ROWS, CHUNK), chosen_blocks, acc, acc2.reshape(NY, NZ, ROWS, WIDTH),
        output_projection_weight,
        adapter_down_weight, adapter_up_weight, post_norm_gain.reshape(1, CHUNK),
        value_head_weight.reshape(1, CHUNK),
    )
    return hidden.reshape(residual.shape), values


def solution(mesh):
    placed = (
        P("seq", None, "head"),
        P(None, "seq", None, "head"),
        P(None, "seq", None, "head"),
        P(None, "seq", None, "head"),
        P("seq", None, "head"),
        P("seq"),
        P(),
        P("seq"),
        P("head", None),
        P("head", None),
        P(),
        P("head"),
        P("head"),
    )
    return jax.shard_map(
        local,
        mesh=mesh,
        in_specs=placed,
        out_specs=(P("seq", None, "head"), P("seq", None)),
        check_vma=False,
    )
```

time: 130 us -> 110 us (0.85)
  Pallas kernels: 118 us -> 103 us
  local copies, waits for them, and re-layouts: 10.9 us -> 6.13 us
    pallas_call x2, Pallas kernels: 89.2 us -> 65.8 us  [the longest x1 51.5 us: local(): pl.pallas_call(finish_kernel, out_shape=(sds((ROWS, CHUNK), BF16), sds((4...]
    pallas_call x1, Pallas kernels: 29 us -> 37 us  [local(): pl.pallas_call(gather_kernel, out_shape=(sds((NY, NZ, ROWS, WIDTH), BF16)...]
    unnamed x27 -> x10, local copies, waits for them, and re-layouts: 10.9 us -> 4.95 us
where the time goes in v2:
time: 110 us
  Pallas kernels  103 us (94%)
  local copies, waits for them, and re-layouts  6.13 us (6%)
    pallas_call x1, Pallas kernels, local(): pl.pallas_call(finish_kernel, out_shape=(sds((ROWS, CHUNK), BF16), sds((4...  51.5 us
    pallas_call x1, Pallas kernels, local(): pl.pallas_call(gather_kernel, out_shape=(sds((NY, NZ, ROWS, WIDTH), BF16)...  37 us
    pallas_call x1, Pallas kernels, local(): pl.pallas_call(functools.partial(prefix_kernel, rc), out_shape=(sds((rows...  14.3 us
    unnamed x10, local copies, waits for them, and re-layouts  4.95 us

profile of v2, /device:TPU:1, one launch (start us, length us, event | category | flops | bytes accessed | tf_op | source)
XLA Modules:
  0.0 109.6 jit_solution(13905111337024643366)
XLA Ops:
  0.6 1.4 %copy.15.map_ref = s32[128,1]{1,0:T(8,128)} copy(s32[128,1]{0,1:T(1,128)} %param.19) | data formatting | bytes 1024 | tf_op args[6]
  2.0 37.0 %gather_queries.1 = (bf16[4,8,64,512]{3,2,1,0:T(8,128)(2,1)}, f32[4,8,64,512]{3,2,1,0:T(8,128)}, f32[4,8,8,128]{3,2,1,0:T(8,128)}, f32[64,512]{1,0:T(8,128)}, f32[64,512]{1,0:T(8,128)}, /*index=5*/s32[16,128]{1,0:T(8,128)}) custom-call(s32[4]{0:T(128)} %len_ref.1, s32[8]{0:T(128)} %slot_ref.5, bf16[64,512]{1,0:T(8,128)(2,1)} %bitcast.13, ...), custom_call_target="tpu_custom_call" | custom-call | tf_op jit(solution)/shard_map/gather_queries/pallas_call | solution.py:761
  39.0 0.0 copy-start
  39.0 0.0 copy-start.1
  39.1 0.0 copy-start.2
  39.1 14.3 %prefix_attention.1 = (f32[2048,512]{1,0:T(8,128)}, f32[32,8,128]{2,1,0:T(8,128)}, bf16[2,2,512,256]{3,2,1,0:T(8,128)(2,1)}) custom-call(s32[8]{0:T(128)} %slot_ref.5, s32[16,128]{1,0:T(8,128)} %get-tuple-element.13.table_ref, bf16[2048,512]{1,0:T(8,128)(2,1)} %bitcast.7, bf16[2,8,512,256]{3,2,1,0:T(8,128)(2,1)} %pool_hbm.1, f32[32,8,128]{2,1,0:T(8,128)} %bitcast.10), custom_call_target="tpu_custom_call" | custom-call | tf_op jit(solution)/shard_map/prefix_attention/pallas_call | solution.py:796
  53.4 0.0 copy-done
  53.4 0.8 copy.16.down_ref
  54.1 0.0 copy-done.1
  54.1 0.6 reshape.37.gain_ref
  54.7 0.0 copy-done.2
  54.7 0.6 reshape.38.vhw_ref
  55.3 51.5 %reduce_and_project.1 = (bf16[64,576]{1,0:T(8,128)(2,1)}, f32[4,16]{1,0:T(4,128)}) custom-call(s32[8]{0:T(128)} %slot_ref.5, f32[4,8,8,128]{3,2,1,0:T(8,128)} %bitcast.9, bf16[4,8,64,512]{3,2,1,0:T(8,128)(2,1)} %get-tuple-element.14.q_ref, f32[64,512]{1,0:T(8,128)} %get-tuple-element.17.oloc, f32[64,512]{1,0:T(8,128)} %get-tuple-element.18.lloc, ...), custom_call_target="tpu_custom_call" | custom-call | tf_op jit(solution)/shard_map/reduce_and_project/pallas_call | solution.py:827
  106.8 1.5 %copy.19 = bf16[4,16,576]{2,1,0:T(8,128)(2,1)} copy(bf16[4,16,576]{2,1,0:T(8,128)(2,1)} %bitcast.11) | data formatting | bytes 147456
  108.3 1.3 %copy.20 = f32[4,16]{1,0:T(4,128)} copy(f32[4,16]{1,0:T(4,128)} %get-tuple-element.27) | data formatting | bytes 512
Async XLA Ops:
  39.0 14.3 %copy-start = (bf16[512,16]{0,1:T(8,128)(2,1)S(1)}, bf16[512,16]{0,1:T(8,128)(2,1)}, u32[]{:S(2)}) copy-start(bf16[512,16]{0,1:T(8,128)(2,1)} %param.22) | copy-start | bytes 49156
  39.0 15.1 %copy-start.1 = (f32[576]{0:T(1024)S(1)}, f32[576]{0:T(1024)}, u32[]{:S(2)}) copy-start(f32[576]{0:T(1024)} %param.24) | copy-start | bytes 6916
  39.1 15.7 %copy-start.2 = (f32[576]{0:T(1024)S(1)}, f32[576]{0:T(1024)}, u32[]{:S(2)}) copy-start(f32[576]{0:T(1024)} %param.25) | copy-start | bytes 6916

commit v3 on v2

--- a/solution.py
+++ b/solution.py
@@ -21,6 +21,7 @@
 HEADS = 4
 CHUNK = 576
 GROUP = 12
+FAR_FIRST = (4, 3, 5, 2, 6, 1, 7, 0)
 PADDED = 640
 MIB = 1 << 20
 K1_MIB, K2_MIB, K3_MIB = 58, 58, 58
@@ -91,32 +92,33 @@
     return dot_t(picker, hi) + dot_t(picker, lo)
 
 
-def system_round(load_q, store, pool, picks, qtmp, sbuf, otmp, lbuf, arrived=None):
-    for m in range(8):
+def system_round(count, load_q, store, pool, picks, qtmp, sbuf, otmp, lbuf, arrived=None):
+    n = count * ROWS
+    for m in range(count):
         qtmp[m * ROWS : (m + 1) * ROWS, :] = load_q(m)
     (b0, v0), (b1, v1) = picks
 
     def score(h, b):
-        return dot_t(qtmp[:, cols(h)], pool[0, b, :, cols(h // 2)])
-
-    sbuf[0] = score(0, b0)
+        return dot_t(qtmp[:n, cols(h)], pool[0, b, :, cols(h // 2)])
+
+    sbuf[0, :n] = score(0, b0)
     for h in range(HEADS):
         g = h // 2
-        sbuf[1] = score(h, b1)
-        p0 = weight_of(sbuf[0])
+        sbuf[1, :n] = score(h, b1)
+        p0 = weight_of(sbuf[0, :n])
         l0 = lane_sum(p0)
         o0 = dot(p0.astype(BF16), pool[1, b0, :, cols(g)])
         if h < HEADS - 1:
-            sbuf[0] = score(h + 1, b0)
-        p1 = weight_of(sbuf[1])
+            sbuf[0, :n] = score(h + 1, b0)
+        p1 = weight_of(sbuf[1, :n])
         l1 = lane_sum(p1)
         o1 = dot(p1.astype(BF16), pool[1, b1, :, cols(g)])
-        otmp[:, cols(h)] = o0 * v0 + o1 * v1
-        lbuf[:, cols(h)] = l0 * v0 + l1 * v1
-    total = head_sums(head_picker(), lbuf[...])
+        otmp[:n, cols(h)] = o0 * v0 + o1 * v1
+        lbuf[:n, cols(h)] = l0 * v0 + l1 * v1
+    total = head_sums(head_picker(), lbuf[:n])
     if arrived is not None:
         arrived()
-    for m in range(8):
+    for m in range(count):
         at = slice(m * ROWS, (m + 1) * ROWS)
         store(m, otmp[at, :], total[:, at])
 
@@ -130,11 +132,21 @@
     core = lax.rem(head, 2)
 
     barrier = pltpu.get_barrier_semaphore()
+
+    def greet(axis, step):
+        pl.semaphore_signal(
+            barrier, inc=1, device_id=shifted(y, z, head, axis, step), device_id_type=MESH
+        )
+
     for axis in (0, 1):
         for step in (1, -1):
-            pl.semaphore_signal(
-                barrier, inc=1, device_id=shifted(y, z, head, axis, step), device_id_type=MESH
-            )
+            greet(axis, step)
+
+    @pl.when(core == 1)
+    def _():
+        greet(1, 2)
+        greet(1, -2)
+
     loads = []
     for i in range(4):
         c = pltpu.make_async_copy(resp_ref.at[:, i], cache.at[i], load_sem.at[i])
@@ -144,11 +156,18 @@
     pool_load.start()
     qall[y, z] = q_ref[...]
     picks = chosen(slot_ref, SYS_BLOCKS, (0, 1))
-    pl.semaphore_wait(barrier, 4)
+
+    @pl.when(core == 0)
+    def _():
+        pl.semaphore_wait(barrier, 4)
+
+    @pl.when(core == 1)
+    def _():
+        pl.semaphore_wait(barrier, 6)
 
     def list_members():
-        task = jnp.broadcast_to(map_ref[...].astype(F32), (HEAD, HEAD))
-        across = jnp.transpose(task)
+        across = jnp.broadcast_to(map_ref[...].astype(F32), (HEAD, HEAD))
+        task = jnp.transpose(across)
         row = lax.broadcasted_iota(jnp.int32, (HEAD, HEAD), 0)
         lane = lax.broadcasted_iota(jnp.int32, (HEAD, HEAD), 1)
         earlier = jnp.where((task == across) & (lane < row), 1.0, 0.0)
@@ -164,35 +183,35 @@
         length = len_ref[i]
         rows = slice(i * 16, (i + 1) * 16)
 
-        def group(g, _):
-            def at(j):
-                return pl.ds(pl.multiple_of((2 * g + j) * HEAD, HEAD), HEAD)
-
-            gc = pl.ds(pl.multiple_of(g * HEAD, HEAD), HEAD)
-            lhs = jnp.concatenate([q_ref[rows, at(0)], q_ref[rows, at(1)]], axis=0)
-            out = jnp.zeros((32, HEAD), F32)
-            total = jnp.zeros((32, HEAD), F32)
-            for part in range(4):
-                keys = slice(part * 512, (part + 1) * 512)
-                p = weight_of(dot_t(lhs, cache[i, 0, keys, gc]))
-                where = lax.broadcasted_iota(jnp.int32, p.shape, 1) + part * 512
-                p = jnp.where(where < length, p, 0.0)
-                total = total + lane_sum(p)
-                out = out + dot(p.astype(BF16), cache[i, 1, keys, gc])
-            p = weight_of(dot_t(lhs, inc_ref[0, i, :, gc]))
-            n = lax.rem(lax.broadcasted_iota(jnp.int32, p.shape, 0), 16)
-            m = lax.broadcasted_iota(jnp.int32, p.shape, 1)
-            p = jnp.where(m <= n, p, 0.0)
-            out = out + dot(p.astype(BF16), inc_ref[1, i, :, gc])
-            wide = jnp.broadcast_to(
-                jnp.sum(total, axis=1, keepdims=True) + jnp.sum(p, axis=1, keepdims=True), (32, HEAD)
-            )
-            for j in range(2):
-                oloc[rows, at(j)] = out[j * 16 : (j + 1) * 16]
-                lloc[rows, at(j)] = wide[j * 16 : (j + 1) * 16]
-            return 0
-
-        lax.fori_loop(0, 2, group, 0)
+        none = jnp.zeros((16, HEAD), BF16)
+        lhs = jnp.concatenate(
+            [
+                jnp.concatenate(
+                    [q_ref[rows, cols(h)], none] if h < 2 else [none, q_ref[rows, cols(h)]], axis=1
+                )
+                for h in range(HEADS)
+            ],
+            axis=0,
+        )
+        p = weight_of(dot_t(lhs, inc_ref[0, i]))
+        n = lax.rem(lax.broadcasted_iota(jnp.int32, p.shape, 0), 16)
+        m = lax.broadcasted_iota(jnp.int32, p.shape, 1)
+        p = jnp.where(m <= n, p, 0.0)
+        total = jnp.zeros((64, HEAD), F32)
+        own = jnp.sum(p, axis=1, keepdims=True)
+        out = dot(p.astype(BF16), inc_ref[1, i])
+        for part in range(4):
+            keys = slice(part * 512, (part + 1) * 512)
+            p = weight_of(dot_t(lhs, cache[i, 0, keys, :]))
+            where = lax.broadcasted_iota(jnp.int32, p.shape, 1) + part * 512
+            p = jnp.where(where < length, p, 0.0)
+            total = total + lane_sum(p)
+            out = out + dot(p.astype(BF16), cache[i, 1, keys, :])
+        wide = jnp.broadcast_to(jnp.sum(total, axis=1, keepdims=True) + own, (64, HEAD))
+        for h in range(HEADS):
+            at = slice(h * 16, (h + 1) * 16)
+            oloc[rows, cols(h)] = out[at, cols(h // 2)]
+            lloc[rows, cols(h)] = wide[at]
 
     def copies(axis1):
         axis2 = 1 - axis1
@@ -211,10 +230,14 @@
 
         def first(d, k):
             s = 1 - 2 * d
-            view = piece(wrap(c1 - s * k, n1), c2, d if k == h1 - 1 else None)
+            if h1 == 2:
+                origin, by = k, 1
+            else:
+                origin, by = 2 * (k // 2), 1 + k % 2
+            view = piece(wrap(c1 - s * origin, n1), c2, d if k == h1 - 1 else None)
             return pltpu.make_async_remote_copy(
                 src_ref=view, dst_ref=view, send_sem=s1.at[d, k], recv_sem=r1.at[d, k],
-                device_id=shifted(y, z, head, axis1, s), device_id_type=MESH,
+                device_id=shifted(y, z, head, axis1, s * by), device_id_type=MESH,
             )
 
         def second(j, d, k):
@@ -225,25 +248,51 @@
                 device_id=shifted(y, z, head, axis2, s), device_id_type=MESH,
             )
 
+        def spread(j):
+            for e in (0, 1):
+                second(j, e, 0).start()
+
         def phase1(work):
-            for d in (0, 1):
-                first(d, 0).start()
-            for d in (0, 1):
-                second(0, d, 0).start()
-            for k in range(h1):
-                for i in work[k]:
-                    attend(i)
-                for d in (0, 1):
-                    first(d, k).wait_recv()
-                    if k < h1 - 1:
-                        first(d, k + 1).start()
-                if k < h1 - 1:
-                    for d in (0, 1):
-                        for e in (0, 1):
-                            second(1 + 2 * k + d, e, 0).start()
-                else:
-                    for e in (0, 1):
-                        second(n1 - 1, e, 0).start()
+            both = (0, 1)
+            if h1 == 2:
+                for d in both:
+                    first(d, 0).start()
+                spread(0)
+                attend(work[0])
+                for d in both:
+                    first(d, 0).wait_recv()
+                    first(d, 1).start()
+                for d in both:
+                    spread(1 + d)
+                attend(work[1])
+                for d in both:
+                    first(d, 1).wait_recv()
+                spread(n1 - 1)
+            else:
+                for k in (1, 0):
+                    for d in both:
+                        first(d, k).start()
+                spread(0)
+                attend(work[0])
+                attend(work[1])
+                for d in both:
+                    first(d, 1).wait_recv()
+                    first(d, 3).start()
+                    first(d, 2).start()
+                for d in both:
+                    first(d, 0).wait_recv()
+                    spread(1 + d)
+                for d in both:
+                    spread(3 + d)
+            attend(work[2])
+            attend(work[3])
+            if h1 != 2:
+                for d in both:
+                    first(d, 2).wait_recv()
+                    spread(5 + d)
+                for d in both:
+                    first(d, 3).wait_recv()
+                spread(n1 - 1)
 
         def forward(k):
             for j in range(n1):
@@ -269,15 +318,11 @@
             action()
 
     def start0():
-        phase1, forward, _ = copies(0)
-        phase1(([0], [1]))
-        attend(2)
-        attend(3)
+        copies(0)[0]((0, 1, 2, 3))
         list_members()
-        forward(0)
 
     def start1():
-        copies(1)[0](([0], [1], [2], [3]))
+        copies(1)[0]((0, 1, 2, 3))
         list_members()
 
     on(0, start0)
@@ -287,12 +332,16 @@
     def keep(at):
         return pltpu.make_async_copy(acc.at[at], acc_out.at[at], acc_sem.at[at])
 
-    def compute(pair, y_step):
+    def compute(count, unit):
         def coords(m):
-            a = wrap(z + pair[m // 4], NZ)
+            u = unit + m // 4
+            k = lax.div(u, 2)
+            odd = lax.rem(u, 2)
+            column = jnp.where(odd == 1, -1 - k, k)
+            row = jnp.where(k == 1, -1, jnp.where(k == 2, 1, jnp.where(k == 3, 2, 0)))
             return (
-                jnp.where(core == 0, m % 4, wrap(y + y_step, NY)),
-                jnp.where(core == 0, a, m),
+                jnp.where(core == 0, m % 4, wrap(y + row, NY)),
+                jnp.where(core == 0, wrap(z + column, NZ), odd * 4 + m % 4),
             )
 
         def load_q(m):
@@ -304,7 +353,7 @@
             keep(at).start()
             sums[at] = jnp.concatenate([total, jnp.zeros((8, HEAD - ROWS), F32)], axis=1)
 
-        system_round(load_q, store, pool, picks, qtmp, sbuf, otmp, lbuf)
+        system_round(count, load_q, store, pool, picks, qtmp, sbuf, otmp, lbuf)
 
     def in_round(r, index, core_index, action):
         @pl.when((r == index) & (core == core_index))
@@ -312,14 +361,21 @@
             action()
 
     def one_round(r, _):
-        compute((r, -1 - r), jnp.where(r == 1, -1, jnp.where(r == 2, 1, jnp.where(r == 3, 2, 0))))
-        for k in range(3):
-            in_round(r, k, 0, lambda: copies(0)[1](k + 1))
+        @pl.when((r == 0) | (r == 4))
+        def _():
+            compute(4, jnp.where(r == 0, 0, 7))
+
+        @pl.when((r > 0) & (r < 4))
+        def _():
+            compute(8, 2 * r - 1)
+
+        for k in range(4):
+            in_round(r, k, 0, lambda: copies(0)[1](k))
         in_round(r, 0, 1, lambda: copies(1)[1](0))
         in_round(r, 2, 1, lambda: copies(1)[1](1))
         return 0
 
-    lax.fori_loop(0, 4, one_round, 0)
+    lax.fori_loop(0, 5, one_round, 0)
     on(0, lambda: copies(0)[2]())
     on(1, lambda: copies(1)[2]())
     for a in range(NY):
@@ -497,12 +553,17 @@
     wcopy.start()
     picks = [(n, v) for n, (_, v) in enumerate(chosen(slot_ref, SYS_BLOCKS, (2, 3)))]
 
-    def compute(pair, y_step, arrived):
+    def compute(count, unit, arrived):
         def coords(m):
-            a = wrap(z + pair[m // 4], NZ)
+            u = unit + m // 4
+            k = lax.div(u, 2)
+            odd = lax.rem(u, 2)
+            column = jnp.where(odd == 1, 3 - k, k - 4)
+            row = jnp.where(k == 0, 2, jnp.where(k == 1, 1, jnp.where(k == 2, -1, 0)))
+            place = jnp.where(odd == 0, FAR_FIRST[m % 4], FAR_FIRST[4 + m % 4])
             return (
-                jnp.where(core == 0, m % 4, wrap(y + y_step, NY)),
-                jnp.where(core == 0, a, m),
+                jnp.where(core == 0, m % 4, wrap(y + row, NY)),
+                jnp.where(core == 0, wrap(z + column, NZ), wrap(z + place, NZ)),
             )
 
         def load_q(m):
@@ -513,7 +574,7 @@
             acc[at] = (acc[at] + acc2[at]) + out
             sums[at] = l_ref[at] + jnp.concatenate([total, jnp.zeros((8, HEAD - ROWS), F32)], axis=1)
 
-        system_round(load_q, store, pool, picks, qtmp, sbuf, otmp, lbuf, arrived)
+        system_round(count, load_q, store, pool, picks, qtmp, sbuf, otmp, lbuf, arrived)
 
     half = ROWS // 2
 
@@ -523,7 +584,8 @@
         c1, c2 = (y, z) if axis1 == 0 else (z, y)
         h = n1 // 2
         rb, rl = (rb_y, rl_y) if axis1 == 0 else (rb_z, rl_z)
-        order = [wrap(c2 + t, n2) for t in list(range(n2 // 2, n2)) + list(range(0, n2 // 2))]
+        turns = sorted(range(1, n2), key=lambda t: -min(t, n2 - t)) + [0]
+        order = [wrap(c2 + t, n2) for t in turns]
 
         def own(i, j):
             return acc[i, j] if axis1 == 0 else acc[j, i]
@@ -551,31 +613,33 @@
                 device_id=shifted(y, z, head, axis1, s), device_id_type=MESH,
             )
 
-        def begin():
-            for j in order:
+        def begin(js):
+            for j in js:
                 far[j] = own(wrap(c1 + h, n1), j).astype(BF16)
                 for d in (0, 1):
                     copy(d, 0, j).start()
-            copy_l(0, 0).start()
-
-        def step(d, k):
-            to = wrap(c1 + (1 - 2 * d) * (h - k), n1)
-            for j in order:
-                copy(d, k - 1, j).wait_recv()
-                here = own(to, j)
-                if k == 1:
-                    a = pl.ds(d * half, half)
-                    b = pl.ds((1 - d) * half, half)
-                    there = rb[d, 0, j, a].astype(F32)
-                    rb[d, 0, j, a] = (there + here[d * half : (d + 1) * half]).astype(BF16)
-                    rb[d, 0, j, b] = here[(1 - d) * half : (2 - d) * half].astype(BF16)
-                else:
-                    rb[d, k - 1, j] = (rb[d, k - 1, j].astype(F32) + here).astype(BF16)
-                copy(d, k, j).start()
-            if k > d:
-                copy_l(d, k - 1).wait_recv()
-                rl[d, k - 1] = rl[d, k - 1] + own_l(to)[...]
-            copy_l(d, k).start()
+
+        def step_l(pairs):
+            for d, k in pairs:
+                if k > d:
+                    copy_l(d, k - 1).wait_recv()
+                    rl[d, k - 1] = rl[d, k - 1] + own_l(wrap(c1 + (1 - 2 * d) * (h - k), n1))[...]
+                copy_l(d, k).start()
+
+        def step(pairs, js):
+            for j in js:
+                for d, k in pairs:
+                    copy(d, k - 1, j).wait_recv()
+                    here = own(wrap(c1 + (1 - 2 * d) * (h - k), n1), j)
+                    if k == 1:
+                        a = pl.ds(d * half, half)
+                        b = pl.ds((1 - d) * half, half)
+                        there = rb[d, 0, j, a].astype(F32)
+                        rb[d, 0, j, a] = (there + here[d * half : (d + 1) * half]).astype(BF16)
+                        rb[d, 0, j, b] = here[(1 - d) * half : (2 - d) * half].astype(BF16)
+                    else:
+                        rb[d, k - 1, j] = (rb[d, k - 1, j].astype(F32) + here).astype(BF16)
+                    copy(d, k, j).start()
 
         def direct(t):
             return pltpu.make_async_remote_copy(
@@ -590,17 +654,6 @@
             )
 
         def final():
-            turns = sorted(range(1, n2), key=lambda t: -min(t, n2 - t)) + [0]
-            for n, t in enumerate(turns):
-                j = wrap(c2 + t, n2)
-                for d in (0, 1):
-                    copy(d, h - 1, j).wait_recv()
-                v = own(c1, j) + rb[0, h - 1, j].astype(F32) + rb[1, h - 1, j].astype(F32)
-                if t == 0:
-                    mine[...] = v
-                else:
-                    part1[t] = v.astype(BF16)
-                    direct(t).start()
             for d in (0, 1):
                 copy_l(d, h - 1).wait_recv()
             for t in turns:
@@ -612,16 +665,28 @@
                 else:
                     lpart1[t] = v
                     direct_l(t).start()
+            for t in turns:
+                j = wrap(c2 + t, n2)
+                for d in (0, 1):
+                    copy(d, h - 1, j).wait_recv()
+                v = own(c1, j) + rb[0, h - 1, j].astype(F32) + rb[1, h - 1, j].astype(F32)
+                if t == 0:
+                    mine[...] = v
+                else:
+                    part1[t] = v.astype(BF16)
+                    direct(t).start()
+            w = small[...]
+            for t in turns[:-1]:
+                direct_l(t).wait_recv()
+                w = w + rl2[t]
+            small[...] = w
             v = mine[...]
-            w = small[...]
             for t in turns[:-1]:
                 direct(t).wait_recv()
                 v = v + rb2[t].astype(F32)
-            for t in turns[:-1]:
-                direct_l(t).wait_recv()
-                w = w + rl2[t]
             mine[...] = v
-            small[...] = w
+
+        def drain():
             for d in (0, 1):
                 for k in range(h):
                     for j in order:
@@ -632,21 +697,40 @@
                 direct(t).wait_send()
                 direct_l(t).wait_send()
 
-        return begin, step, final
-
-    def steps(axis1, pairs):
-        step = ring(axis1)[1]
-        for d, k in pairs:
-            step(d, k)
+        return begin, step, step_l, final, drain, order
+
+    def after0(r):
+        begin, step, step_l, _, _, order = ring(1)
+        if r == 0:
+            pl.semaphore_wait(barrier, NH - 1 + 2 + NY - 1)
+            step_l(((0, 0),))
+            begin(order)
+        else:
+            step_l(((0, r), (1, r)))
+            step(((0, r), (1, r)), order)
+
+    def after1(r):
+        begin, step, step_l, _, _, order = ring(0)
+        a, b = order[:4], order[4:]
+        if r == 0:
+            pl.semaphore_wait(barrier, NH - 1 + 2 + NZ - 1)
+            begin(a)
+        elif r == 1:
+            step_l(((0, 0),))
+            begin(b)
+            step(((0, 1),), a)
+        elif r == 2:
+            step_l(((0, 1),))
+            step(((0, 1),), b)
+            step(((1, 1),), a)
+        else:
+            step_l(((1, 1),))
+            step(((1, 1),), b)
 
     def in_round(r, index, core_index, action):
         @pl.when((r == index) & (core == core_index))
         def _():
             action()
-
-    def start(axis1, direct):
-        pl.semaphore_wait(barrier, NH - 1 + 2 + direct - 1)
-        ring(axis1)[0]()
 
     def arrived_in(r):
         @pl.when(r == 0)
@@ -655,62 +739,81 @@
                 x.wait()
 
     def one_round(r, _):
-        y_step = jnp.where(r == 0, 2, jnp.where(r == 1, 1, jnp.where(r == 2, -1, 0)))
-        compute((r - 4, 3 - r), y_step, lambda: arrived_in(r))
-        in_round(r, 0, 0, lambda: start(1, NY))
-        in_round(r, 0, 1, lambda: start(0, NZ))
-        for k in range(1, 4):
-            in_round(r, k, 0, lambda: steps(1, ((0, k), (1, k))))
-        in_round(r, 1, 1, lambda: steps(0, ((0, 1),)))
-        in_round(r, 2, 1, lambda: steps(0, ((1, 1),)))
+        @pl.when((r == 0) | (r == 4))
+        def _():
+            compute(4, jnp.where(r == 0, 0, 7), lambda: arrived_in(r))
+
+        @pl.when((r > 0) & (r < 4))
+        def _():
+            compute(8, 2 * r - 1, None)
+
+        for k in range(4):
+            in_round(r, k, 0, lambda: after0(k))
+            in_round(r, k, 1, lambda: after1(k))
         return 0
 
-    lax.fori_loop(0, 4, one_round, 0)
-    on(0, lambda: ring(1)[2]())
-    on(1, lambda: ring(0)[2]())
-
-    sums = jnp.transpose(jnp.concatenate([small[...], jnp.zeros((HEAD - 8, HEAD), F32)], axis=0))
+    lax.fori_loop(0, 5, one_round, 0)
+    on(0, lambda: ring(1)[3]())
+    on(1, lambda: ring(0)[3]())
+
+    rows_sum = jnp.transpose(jnp.concatenate([small[...], jnp.zeros((HEAD - 8, HEAD), F32)], axis=0))
     att = []
     for h in range(HEADS):
-        den = sums[:ROWS, h : h + 1] + lloc[:, cols(h)]
+        den = rows_sum[:ROWS, h : h + 1] + lloc[:, cols(h)]
         att.append(((mine[:, cols(h)] + oloc[:, cols(h)]) / den).astype(BF16))
     att = jnp.concatenate(att, axis=1)
-    low = dot(att, down_ref[...])
+    low = dot_t(att, down_ref[...])
     low_hi = low.astype(BF16)
     low_lo = (low - low_hi.astype(F32)).astype(BF16)
     low_lo2 = (low - low_hi.astype(F32) - low_lo.astype(F32)).astype(BF16)
+    low3 = jnp.concatenate([low_hi, low_lo, low_lo2], axis=1)
     wcopy.wait()
-    sends = {}
-    for t in (4, 3, 5, 2, 6, 1, 7, 0):
-        to = wrap(head + t, NH)
+    def project(to):
         odd = lax.rem(to, 2)
         at = pl.ds(pl.multiple_of(to * CHUNK - odd * (HEAD // 2), HEAD), PADDED)
         u = up_ref[:, at]
-        v = dot(att, wbuf[:, at]) + (dot(low_hi, u) + dot(low_lo, u) + dot(low_lo2, u))
-        v = jnp.where(odd == 1, v[:, HEAD // 2 :], v[:, :CHUNK])
+        v = dot(att, wbuf[:, at]) + dot(low3, jnp.concatenate([u, u, u], axis=0))
+        return jnp.where(odd == 1, v[:, HEAD // 2 :], v[:, :CHUNK])
+
+    x_here = lax.div(head, 2)
+    sends = []
+    for t in (2, 1, 3, 0):
+        chunk[t] = project(2 * wrap(x_here + t, NH // 2) + 1 - core).astype(BF16)
+        x = pltpu.make_async_remote_copy(
+            src_ref=chunk.at[t], dst_ref=rchunk.at[t], send_sem=hs.at[t], recv_sem=hr.at[t],
+            device_id=(seq, 2 * x_here + 1 - core), device_id_type=MESH,
+        )
+        x.start()
+        sends.append(x)
+    across = {}
+    for n, t in enumerate((2, 1, 3, 0)):
+        v = project(2 * wrap(x_here + t, NH // 2) + core)
+        sends[n].wait_recv()
+        v = v + rchunk[t].astype(F32)
         if t == 0:
             pmine[...] = v
             continue
-        chunk[t - 1] = v.astype(BF16)
+        chunk[3 + t] = v.astype(BF16)
         x = pltpu.make_async_remote_copy(
-            src_ref=chunk.at[t - 1], dst_ref=rchunk.at[t - 1], send_sem=hs.at[t - 1], recv_sem=hr.at[t - 1],
-            device_id=(seq, to), device_id_type=MESH,
+            src_ref=chunk.at[3 + t], dst_ref=rchunk.at[3 + t], send_sem=hs.at[3 + t], recv_sem=hr.at[3 + t],
+            device_id=(seq, 2 * wrap(x_here + t, NH // 2) + core), device_id_type=MESH,
         )
         x.start()
-        sends[t] = x
+        across[t] = x
+        sends.append(x)
     p = pmine[...]
-    for t in (1, 7, 2, 6, 3, 5, 4):
-        sends[t].wait_recv()
-        p = p + rchunk[t - 1].astype(F32)
+    for t in (1, 3, 2):
+        across[t].wait_recv()
+        p = p + rchunk[3 + t].astype(F32)
 
     res = res_ref[...].astype(F32)
-    gain = gain_ref[...]
-    vhw = vhw_ref[...]
+    gain = gain_ref[...].reshape(1, CHUNK)
+    vhw = vhw_ref[...].reshape(1, CHUNK)
     pg = p * gain
-    parts = [p * p, res * res, res * pg, pg * pg, res * vhw, pg * vhw]
+    terms = [p * p, res * res, res * pg, pg * pg, res * vhw, pg * vhw]
     lane = lax.broadcasted_iota(jnp.int32, (ROWS, HEAD), 1)
     packed = jnp.zeros((ROWS, HEAD), F32)
-    for i, v in enumerate(parts):
+    for i, v in enumerate(terms):
         packed = jnp.where(lane == i, jnp.sum(v, axis=1, keepdims=True), packed)
     packed = jnp.concatenate([packed, jnp.zeros((HEAD - ROWS, HEAD), F32)], axis=0)
     small[...] = jnp.transpose(packed)[:8]
@@ -734,8 +837,10 @@
         val_ref[i : i + 1, :] = value[:, i * 16 : (i + 1) * 16]
     rcol = jnp.transpose(jnp.broadcast_to(r, (HEAD, HEAD)))[:ROWS, :1]
     hid_ref[...] = (res + pg * rcol).astype(BF16)
-    for x in list(sends.values()) + sends2:
+    for x in sends + sends2:
         x.wait_send()
+    on(0, lambda: ring(1)[4]())
+    on(1, lambda: ring(0)[4]())
 
 
 def local(
@@ -789,7 +894,7 @@
         name="gather_queries",
     )(
         lengths, slot_block_table, queries.reshape(ROWS, WIDTH), incoming_key_value,
-        rollout_task_map, response_key_value, prefix_key_value_pool,
+        rollout_task_map.reshape(1, -1), response_key_value, prefix_key_value_pool,
     )
 
     rc = 1024
@@ -873,8 +978,7 @@
         slot_block_table, sums2.reshape(NY, NZ, 8, HEAD), qall, oloc, lloc,
         residual.reshape(ROWS, CHUNK), chosen_blocks, acc, acc2.reshape(NY, NZ, ROWS, WIDTH),
         output_projection_weight,
-        adapter_down_weight, adapter_up_weight, post_norm_gain.reshape(1, CHUNK),
-        value_head_weight.reshape(1, CHUNK),
+        adapter_down_weight.T, adapter_up_weight, post_norm_gain, value_head_weight,
     )
     return hidden.reshape(residual.shape), values
 

time: 110 us -> 106 us (0.964)
  local copies, waits for them, and re-layouts: 6.13 us -> 2.78 us
    pallas_call x1, Pallas kernels: 51.5 us -> 54.2 us  [local(): pl.pallas_call(finish_kernel, out_shape=(sds((ROWS, CHUNK), BF16), sds((4...]
    unnamed x10 -> x2, local copies, waits for them, and re-layouts: 4.95 us -> 2.78 us
    pallas_call x1, Pallas kernels: 37 us -> 35.1 us  [local(): pl.pallas_call(gather_kernel, out_shape=(sds((NY, NZ, ROWS, WIDTH), BF16)...]
    pallas_call x1, Pallas kernels: 14.3 us -> 12.9 us  [local(): pl.pallas_call(functools.partial(prefix_kernel, rc), out_shape=(sds((rows...]
    reshape x2 -> x0, local copies, waits for them, and re-layouts: 1.18 us -> none  [the longest x1 0.6 us: local(): value_head_weight.reshape(1, CHUNK)]
where the time goes in v3:
time: 106 us
  Pallas kernels  102 us (96%)
  local copies, waits for them, and re-layouts  2.78 us (3%)
    pallas_call x1, Pallas kernels, local(): pl.pallas_call(finish_kernel, out_shape=(sds((ROWS, CHUNK), BF16), sds((4...  54.2 us
    pallas_call x1, Pallas kernels, local(): pl.pallas_call(gather_kernel, out_shape=(sds((NY, NZ, ROWS, WIDTH), BF16)...  35.1 us
    pallas_call x1, Pallas kernels, local(): pl.pallas_call(functools.partial(prefix_kernel, rc), out_shape=(sds((rows...  12.9 us
    unnamed x2, local copies, waits for them, and re-layouts  2.78 us

profile of v3, /device:TPU:1, one launch (start us, length us, event | category | flops | bytes accessed | tf_op | source)
XLA Modules:
  0.0 105.6 jit_solution(8599169841842359203)
XLA Ops:
  0.6 35.1 %gather_queries.1 = (bf16[4,8,64,512]{3,2,1,0:T(8,128)(2,1)}, f32[4,8,64,512]{3,2,1,0:T(8,128)}, f32[4,8,8,128]{3,2,1,0:T(8,128)}, f32[64,512]{1,0:T(8,128)}, f32[64,512]{1,0:T(8,128)}, /*index=5*/s32[16,128]{1,0:T(8,128)}) custom-call(s32[4]{0:T(128)} %len_ref.1, s32[8]{0:T(128)} %slot_ref.5, bf16[64,512]{1,0:T(8,128)(2,1)} %bitcast.15, ...), custom_call_target="tpu_custom_call" | custom-call | tf_op jit(solution)/shard_map/gather_queries/pallas_call | solution.py:866
  35.7 12.9 %prefix_attention.1 = (f32[2048,512]{1,0:T(8,128)}, f32[32,8,128]{2,1,0:T(8,128)}, bf16[2,2,512,256]{3,2,1,0:T(8,128)(2,1)}) custom-call(s32[8]{0:T(128)} %slot_ref.5, s32[16,128]{1,0:T(8,128)} %get-tuple-element.13.table_ref, bf16[2048,512]{1,0:T(8,128)(2,1)} %bitcast.9, bf16[2,8,512,256]{3,2,1,0:T(8,128)(2,1)} %pool_hbm.1, f32[32,8,128]{2,1,0:T(8,128)} %bitcast.12), custom_call_target="tpu_custom_call" | custom-call | tf_op jit(solution)/shard_map/prefix_attention/pallas_call | solution.py:901
  48.7 54.2 %reduce_and_project.1 = (bf16[64,576]{1,0:T(8,128)(2,1)}, f32[4,16]{1,0:T(4,128)}) custom-call(s32[8]{0:T(128)} %slot_ref.5, f32[4,8,8,128]{3,2,1,0:T(8,128)} %bitcast.11, bf16[4,8,64,512]{3,2,1,0:T(8,128)(2,1)} %get-tuple-element.14.q_ref, f32[64,512]{1,0:T(8,128)} %get-tuple-element.17.oloc, f32[64,512]{1,0:T(8,128)} %get-tuple-element.18.lloc, ...), custom_call_target="tpu_custom_call" | custom-call | tf_op jit(solution)/shard_map/reduce_and_project/pallas_call | solution.py:932
  102.8 1.5 %copy.17 = bf16[4,16,576]{2,1,0:T(8,128)(2,1)} copy(bf16[4,16,576]{2,1,0:T(8,128)(2,1)} %bitcast.13) | data formatting | bytes 147456
  104.3 1.3 %copy.18 = f32[4,16]{1,0:T(4,128)} copy(f32[4,16]{1,0:T(4,128)} %get-tuple-element.27) | data formatting | bytes 512

commit v4 on v3

--- a/solution.py
+++ b/solution.py
@@ -125,8 +125,8 @@
 
 def gather_kernel(
     len_ref, slot_ref, q_ref, inc_ref, map_ref, resp_ref, pool_ref,
-    qall, acc_out, sums, oloc, lloc, table,
-    cache, pool, acc, qtmp, sbuf, otmp, lbuf, load_sem, pool_sem, acc_sem, s1, r1, s2, r2,
+    q_out, acc_out, sums, oloc, lloc, table,
+    qall, cache, pool, acc, qtmp, sbuf, otmp, lbuf, load_sem, pool_sem, q_sem, acc_sem, s1, r1, s2, r2,
 ):
     y, z, head = position()
     core = lax.rem(head, 2)
@@ -329,6 +329,8 @@
     on(1, start1)
     pool_load.wait()
 
+    q_store = pltpu.make_async_copy(qall, q_out, q_sem)
+
     def keep(at):
         return pltpu.make_async_copy(acc.at[at], acc_out.at[at], acc_sem.at[at])
 
@@ -373,6 +375,11 @@
             in_round(r, k, 0, lambda: copies(0)[1](k))
         in_round(r, 0, 1, lambda: copies(1)[1](0))
         in_round(r, 2, 1, lambda: copies(1)[1](1))
+
+        @pl.when(r == 3)
+        def _():
+            q_store.start()
+
         return 0
 
     lax.fori_loop(0, 5, one_round, 0)
@@ -381,12 +388,15 @@
     for a in range(NY):
         for b in range(NZ):
             keep((a, b)).wait()
+    q_store.wait()
 
 
 def prefix_kernel(
-    rc, slot_ref, table_ref, q_ref, pool_hbm, lin_ref, acc_out, l_ref, sel,
-    pool_ref, acc, lanes, sbuf, qbuf, obuf, lbuf, system, item_slot, item_prompt, item_part, pool_sem, acc_sem,
+    rc, slot_ref, table_ref, q_hbm, pool_hbm, lin_ref, acc_out, l_ref, sel,
+    q_ref, pool_ref, acc, lanes, sbuf, qbuf, obuf, lbuf, system, item_slot, item_prompt, item_part, q_sem, pool_sem, acc_sem,
 ):
+    q_load = pltpu.make_async_copy(q_hbm, q_ref, q_sem)
+    q_load.start()
     pool_load = pltpu.make_async_copy(pool_hbm, pool_ref, pool_sem)
     pool_load.start()
     slots = slot_ref.shape[0]
@@ -420,6 +430,7 @@
 
     acc[...] = jnp.zeros_like(acc)
     lanes[...] = jnp.zeros_like(lanes)
+    q_load.wait()
     pool_load.wait()
     for n in range(2):
         for kv in range(2):
@@ -514,12 +525,14 @@
 
 
 def finish_kernel(
-    slot_ref, l_ref, q_ref, oloc, lloc, res_ref, pool, first_ref, second_ref, w_ref, down_ref, up_ref, gain_ref, vhw_ref,
+    slot_ref, l_ref, q_hbm, oloc, lloc, res_ref, pool, first_ref, second_ref, w_ref, down_ref, up_ref, gain_ref, vhw_ref,
     hid_ref, val_ref,
-    wbuf, acc, acc2, sums, far, qtmp, sbuf, otmp, lbuf, part1, lpart1, mine, pmine,
+    q_ref, wbuf, acc, acc2, sums, far, qtmp, sbuf, otmp, lbuf, part1, lpart1, mine, pmine,
     rb_y, rb_z, rl_y, rl_z, rb2, rl2, chunk, rchunk, small, rsmall,
-    w_sem, a_sem, s1, r1, t1, u1, s2, r2, t2, u2, hs, hr, ss, sr,
+    q_sem, w_sem, a_sem, s1, r1, t1, u1, s2, r2, t2, u2, hs, hr, ss, sr,
 ):
+    q_load = pltpu.make_async_copy(q_hbm, q_ref, q_sem)
+    q_load.start()
     y, z, head = position()
     core = lax.rem(head, 2)
     seq = y * NZ + z
@@ -550,7 +563,6 @@
     for x in parts:
         x.start()
     wcopy = pltpu.make_async_copy(w_ref, wbuf, w_sem)
-    wcopy.start()
     picks = [(n, v) for n, (_, v) in enumerate(chosen(slot_ref, SYS_BLOCKS, (2, 3)))]
 
     def compute(count, unit, arrived):
@@ -732,11 +744,14 @@
         def _():
             action()
 
+    q_load.wait()
+
     def arrived_in(r):
         @pl.when(r == 0)
         def _():
             for x in parts:
                 x.wait()
+            wcopy.start()
 
     def one_round(r, _):
         @pl.when((r == 0) | (r == 4))
@@ -874,13 +889,15 @@
             sds((16, HEAD), jnp.int32),
         ),
         in_specs=[smem, smem, vmem, vmem, vmem, hbm, hbm],
-        out_specs=(vmem, hbm, vmem, vmem, vmem, vmem),
+        out_specs=(hbm, hbm, vmem, vmem, vmem, vmem),
         scratch_shapes=[
+            pltpu.VMEM((NY, NZ, ROWS, WIDTH), BF16),
             pltpu.VMEM((4, 2, 2048, 256), BF16),
             pool_buf,
             pltpu.VMEM((NY, NZ, ROWS, WIDTH), F32),
             *round_bufs,
             dma((4,)),
+            dma(()),
             dma(()),
             dma((NY, NZ)),
             dma((2, NZ // 2)),
@@ -905,9 +922,10 @@
             sds((devices, 8, HEAD), F32),
             sds((2, 2, 512, 256), BF16),
         ),
-        in_specs=[smem, smem, vmem, hbm, vmem],
+        in_specs=[smem, smem, hbm, hbm, vmem],
         out_specs=(hbm, vmem, vmem),
         scratch_shapes=[
+            pltpu.VMEM((rows_all, WIDTH), BF16),
             pool_buf,
             pltpu.VMEM((rows_all, WIDTH), F32),
             pltpu.VMEM((rows_all, WIDTH), F32),
@@ -921,6 +939,7 @@
             pltpu.SMEM((24,), jnp.int32),
             dma(()),
             dma(()),
+            dma(()),
         ],
         compiler_params=pltpu.CompilerParams(vmem_limit_bytes=K2_MIB * MIB),
         name="prefix_attention",
@@ -932,9 +951,10 @@
     hidden, values = pl.pallas_call(
         finish_kernel,
         out_shape=(sds((ROWS, CHUNK), BF16), sds((4, 16), F32)),
-        in_specs=[smem] + [vmem] * 6 + [hbm] * 3 + [vmem] * 4,
+        in_specs=[smem, vmem, hbm] + [vmem] * 4 + [hbm] * 3 + [vmem] * 4,
         out_specs=(vmem, vmem),
         scratch_shapes=[
+            pltpu.VMEM((NY, NZ, ROWS, WIDTH), BF16),
             pltpu.VMEM((WIDTH, MODEL_WIDTH), BF16),
             pltpu.VMEM((NY, NZ, ROWS, WIDTH), F32),
             pltpu.VMEM((NY, NZ, ROWS, WIDTH), F32),
@@ -955,6 +975,7 @@
             pltpu.VMEM((NH - 1, ROWS, CHUNK), BF16),
             pltpu.VMEM((8, HEAD), F32),
             pltpu.VMEM((NH - 1, 8, HEAD), F32),
+            dma(()),
             dma(()),
             dma((2,)),
             dma((2, NZ // 2, NZ)),

time: 106 us -> 103 us (0.972)
  Pallas kernels: 102 us -> 99.6 us
    pallas_call x1, Pallas kernels: 12.9 us -> 10.8 us  [local(): pl.pallas_call(functools.partial(prefix_kernel, rc), out_shape=(sds((rows...]
where the time goes in v4:
time: 103 us
  Pallas kernels  99.6 us (97%)
  local copies, waits for them, and re-layouts  2.78 us (3%)
    pallas_call x1, Pallas kernels, local(): pl.pallas_call(finish_kernel, out_shape=(sds((ROWS, CHUNK), BF16), sds((4...  54.5 us
    pallas_call x1, Pallas kernels, local(): pl.pallas_call(gather_kernel, out_shape=(sds((NY, NZ, ROWS, WIDTH), BF16)...  34.3 us
    pallas_call x1, Pallas kernels, local(): pl.pallas_call(functools.partial(prefix_kernel, rc), out_shape=(sds((rows...  10.8 us
    unnamed x2, local copies, waits for them, and re-layouts  2.78 us

profile of v4, /device:TPU:1, one launch (start us, length us, event | category | flops | bytes accessed | tf_op | source)
XLA Modules:
  0.0 103.0 jit_solution(15535222967577821322)
XLA Ops:
  0.6 34.3 %gather_queries.1 = (bf16[4,8,64,512]{3,2,1,0:T(8,128)(2,1)}, f32[4,8,64,512]{3,2,1,0:T(8,128)}, f32[4,8,8,128]{3,2,1,0:T(8,128)}, f32[64,512]{1,0:T(8,128)}, f32[64,512]{1,0:T(8,128)}, /*index=5*/s32[16,128]{1,0:T(8,128)}) custom-call(s32[4]{0:T(128)} %len_ref.1, s32[8]{0:T(128)} %slot_ref.5, bf16[64,512]{1,0:T(8,128)(2,1)} %bitcast.15, ...), custom_call_target="tpu_custom_call" | custom-call | tf_op jit(solution)/shard_map/gather_queries/pallas_call | solution.py:881
  35.0 10.8 %prefix_attention.1 = (f32[2048,512]{1,0:T(8,128)}, f32[32,8,128]{2,1,0:T(8,128)}, bf16[2,2,512,256]{3,2,1,0:T(8,128)(2,1)}) custom-call(s32[8]{0:T(128)} %slot_ref.5, s32[16,128]{1,0:T(8,128)} %get-tuple-element.13.table_ref, bf16[2048,512]{1,0:T(8,128)(2,1)} %bitcast.9, bf16[2,8,512,256]{3,2,1,0:T(8,128)(2,1)} %pool_hbm.1, f32[32,8,128]{2,1,0:T(8,128)} %bitcast.12), custom_call_target="tpu_custom_call" | custom-call | tf_op jit(solution)/shard_map/prefix_attention/pallas_call | solution.py:918
  45.7 54.5 %reduce_and_project.1 = (bf16[64,576]{1,0:T(8,128)(2,1)}, f32[4,16]{1,0:T(4,128)}) custom-call(s32[8]{0:T(128)} %slot_ref.5, f32[4,8,8,128]{3,2,1,0:T(8,128)} %bitcast.11, bf16[4,8,64,512]{3,2,1,0:T(8,128)(2,1)} %get-tuple-element.14.q_hbm, f32[64,512]{1,0:T(8,128)} %get-tuple-element.17.oloc, f32[64,512]{1,0:T(8,128)} %get-tuple-element.18.lloc, ...), custom_call_target="tpu_custom_call" | custom-call | tf_op jit(solution)/shard_map/reduce_and_project/pallas_call | solution.py:951
  100.2 1.5 %copy.17 = bf16[4,16,576]{2,1,0:T(8,128)(2,1)} copy(bf16[4,16,576]{2,1,0:T(8,128)(2,1)} %bitcast.13) | data formatting | bytes 147456
  101.8 1.3 %copy.18 = f32[4,16]{1,0:T(4,128)} copy(f32[4,16]{1,0:T(4,128)} %get-tuple-element.27) | data formatting | bytes 512
